TPU v7x, 32 devices: a whole 2x2x4 slice. The times are simulated.
32 devices in a mesh: dp: 2 (over x), blk: 4 (over z), head: 4 (over y, core).
Axes of the slice: x: 2, y: 2, z: 4, core: 2. Of those that a mesh axis runs over, the one named last changes fastest.
Arguments:
- tokens: bfloat16 [2, 2048, 768], P('dp', ('blk', 'head')), may hold values from -6 to 6
- order: int32 [2, 2048], P('dp', ('blk', 'head')), may hold values from 0 to 2047, each once within a row
- expert_ids: int32 [2, 2048, 1], replicated, may hold values from 0 to 7
- norm1_gain: bfloat16 [768], P(('dp', 'blk', 'head')), may hold values from 0.5 to 1.5
- w_query: bfloat16 [768, 768], P(('dp', 'blk', 'head')), may hold values from -0.3125 to 0.3125
- w_key: bfloat16 [768, 768], P(('dp', 'blk', 'head')), may hold values from -0.3125 to 0.3125
- w_value: bfloat16 [768, 768], P(('dp', 'blk', 'head')), may hold values from -0.21875 to 0.21875
- w_attn_out: bfloat16 [768, 768], P(('dp', 'blk', 'head')), may hold values from -1.25 to 1.25
- rel_table: bfloat16 [384], P(('dp', 'blk', 'head')), may hold values from -3 to 3
- norm2_gain: bfloat16 [768], P(('dp', 'blk', 'head')), may hold values from 0.5 to 1.5
- w_router: bfloat16 [768, 8], P(('dp', 'blk', 'head')), may hold values from -0.15625 to 0.15625
- w_in: bfloat16 [8, 768, 3072], P(('dp', 'blk')), may hold values from -0.21875 to 0.21875
- w_out: bfloat16 [8, 3072, 768], P(('dp', 'blk')), may hold values from -3.5 to 3.5
- cotangent: bfloat16 [2, 2048, 768], P('dp', ('blk', 'head')), may hold values from -6 to 6
Outputs:
- layer_out: bfloat16 [2, 2048, 768], P('dp', ('blk', 'head'))
- grad_tokens: bfloat16 [2, 2048, 768], P('dp', ('blk', 'head'))
- grad_norm1_gain: float32 [768], P(('dp', 'blk', 'head'))
- grad_w_query: float32 [768, 768], P(('dp', 'blk', 'head'))
- grad_w_key: float32 [768, 768], P(('dp', 'blk', 'head'))
- grad_w_value: float32 [768, 768], P(('dp', 'blk', 'head'))
- grad_w_attn_out: float32 [768, 768], P(('dp', 'blk', 'head'))
- grad_rel_table: float32 [384], P(('dp', 'blk', 'head'))
- grad_norm2_gain: float32 [768], P(('dp', 'blk', 'head'))
- grad_w_router: float32 [768, 8], P(('dp', 'blk', 'head'))
- grad_w_in: float32 [8, 768, 3072], P(('dp', 'blk'))
- grad_w_out: float32 [8, 3072, 768], P(('dp', 'blk'))
Inputs may be any that keep to these rules, and one draw needn't show every extreme that they name: `expert_ids`: every expert is named by some token. `order`: within each sequence every value appears once.
All inputs are finite; a program needn't handle non-finite values.
Results may differ from a plain program's by a relative error of at most 0.033.
Values may be sent and summed in bfloat16 or wider, within the bound.
A program may use at most 192 MiB of HBM per device.

v0:
```python
import jax
import jax.numpy as jnp
from jax import lax
from jax.sharding import PartitionSpec as P

HEAD_COUNT = 12
HEAD_SIZE = 64
BUCKETS = 32
BLOCK = 256


EPSILON = 1e-06
AUX_WEIGHT = 1.0
MASKED = -1e30
INV_ROOT_TWO = 0.7071067811865476
INV_ROOT_TWO_PI = 0.3989422804014327
LIMITS = (1, 2, 3, 4, 5, 6, 7, 8, 12, 16, 23, 32, 46, 64, 91)


def bucket_of(distance, half_count):
    magnitude = jnp.abs(distance)
    bucket = jnp.zeros(distance.shape, jnp.int32)
    for threshold in LIMITS:
        bucket = bucket + (magnitude >= threshold).astype(jnp.int32)
    return bucket + half_count * (distance > 0).astype(jnp.int32)


def gelu_slope(values):
    return (
        0.5 * (1.0 + lax.erf(values * INV_ROOT_TWO))
        + values * jnp.exp(-0.5 * values * values) * INV_ROOT_TWO_PI
    )


def bias_square(table_heads, offset, block_rows):
    bucket_total = table_heads.shape[1]
    slot_ids = jnp.arange(2 * block_rows, dtype=jnp.int32)
    distance = offset + jnp.where(slot_ids < block_rows, slot_ids, slot_ids - 2 * block_rows)
    one_hot = (
        bucket_of(distance, bucket_total // 2)[None, :]
        == jnp.arange(bucket_total, dtype=jnp.int32)[:, None]
    ).astype(jnp.float32)
    bias_line = jnp.dot(table_heads, one_hot, precision=lax.Precision.HIGHEST)
    head_total = bias_line.shape[0]
    repeated = jnp.broadcast_to(
        bias_line[:, None, :], (head_total, block_rows, 2 * block_rows)
    ).reshape(head_total, 2 * block_rows * block_rows)
    skewed = repeated[:, : block_rows * (2 * block_rows - 1)].reshape(
        head_total, block_rows, 2 * block_rows - 1
    )
    return skewed[:, :, :block_rows]


def masked_scores(query_rows, key_rows, bias_block, query_start, key_start, mask_block):
    block_rows = query_rows.shape[0]
    scaling = query_rows.shape[-1] ** (-0.5)
    raw_scores = jnp.einsum(
        "qhd,khd->hqk", query_rows, key_rows, preferred_element_type=jnp.float32
    )
    scores = raw_scores * scaling + bias_block
    query_pos = query_start + jnp.arange(block_rows, dtype=jnp.int32)
    key_pos = key_start + jnp.arange(block_rows, dtype=jnp.int32)
    allowed = key_pos[None, :] // mask_block <= query_pos[:, None] // mask_block
    return jnp.where(allowed[None], scores, MASKED)


def attend_forward(query_rows, key_blocks, value_blocks, table_heads, query_start, mask_block):
    block_rows, head_total, head_dim = query_rows.shape
    block_total = key_blocks.shape[0]
    last_block = (query_start + block_rows - 1) // mask_block

    def scores_at(block_index):
        key_start = block_index * block_rows
        bias_block = bias_square(table_heads, key_start - query_start, block_rows)
        return masked_scores(
            query_rows, key_blocks[block_index], bias_block, query_start, key_start, mask_block
        )

    def live_at(block_index):
        return block_index * block_rows // mask_block <= last_block

    def total_step(state, block_index):

        def total_update(current):
            running_max, running_sum = current
            scores = scores_at(block_index)
            new_max = jnp.maximum(running_max, jnp.max(scores, axis=-1))
            new_sum = running_sum * jnp.exp(running_max - new_max) + jnp.sum(
                jnp.exp(scores - new_max[..., None]), axis=-1
            )
            return (new_max, new_sum)

        return (lax.cond(live_at(block_index), total_update, lambda current: current, state), None)

    start_state = (
        jnp.full((head_total, block_rows), MASKED, jnp.float32),
        jnp.zeros((head_total, block_rows), jnp.float32),
    )
    (running_max, running_sum), unused = lax.scan(
        total_step, start_state, jnp.arange(block_total, dtype=jnp.int32)
    )
    log_total = running_max + jnp.log(running_sum)

    def output_step(acc_sum, block_index):

        def output_update(current):
            soft_weights = jnp.exp(scores_at(block_index) - log_total[..., None]).astype(
                jnp.bfloat16
            )
            return current + jnp.einsum(
                "hqk,khd->qhd",
                soft_weights,
                value_blocks[block_index],
                preferred_element_type=jnp.float32,
            )

        return (
            lax.cond(live_at(block_index), output_update, lambda current: current, acc_sum),
            None,
        )

    output, unused = lax.scan(
        output_step,
        jnp.zeros((block_rows, head_total, head_dim), jnp.float32),
        jnp.arange(block_total, dtype=jnp.int32),
    )
    return (output.astype(jnp.bfloat16), log_total)


def attend_backward(
    query_rows,
    key_blocks,
    value_blocks,
    table_heads,
    log_total,
    grad_rows,
    query_start,
    mask_block,
    grad_keys,
    grad_values,
    grad_table,
):
    block_rows, head_total, head_dim = query_rows.shape
    block_total = key_blocks.shape[0]
    last_block = (query_start + block_rows - 1) // mask_block
    scaling = head_dim ** (-0.5)

    def live_at(block_index):
        return block_index * block_rows // mask_block <= last_block

    def weights_at(block_index, bias_block):
        scores = masked_scores(
            query_rows,
            key_blocks[block_index],
            bias_block,
            query_start,
            block_index * block_rows,
            mask_block,
        )
        return jnp.exp(scores - log_total[..., None])

    def delta_step(delta_sum, block_index):

        def delta_update(current):
            bias_block = bias_square(
                table_heads, block_index * block_rows - query_start, block_rows
            )
            soft_weights = weights_at(block_index, bias_block)
            grad_weights = jnp.einsum(
                "qhd,khd->hqk",
                grad_rows,
                value_blocks[block_index],
                preferred_element_type=jnp.float32,
            )
            return current + jnp.sum(soft_weights * grad_weights, axis=-1)

        return (
            lax.cond(live_at(block_index), delta_update, lambda current: current, delta_sum),
            None,
        )

    delta_sum, unused = lax.scan(
        delta_step,
        jnp.zeros((head_total, block_rows), jnp.float32),
        jnp.arange(block_total, dtype=jnp.int32),
    )

    def grad_step(state, block_index):

        def grad_update(current):
            grad_query, keys_acc, values_acc, table_acc = current
            key_start = block_index * block_rows
            bias_block, bias_pull = jax.vjp(
                lambda table_part: bias_square(table_part, key_start - query_start, block_rows),
                table_heads,
            )
            soft_weights = weights_at(block_index, bias_block)
            grad_weights = jnp.einsum(
                "qhd,khd->hqk",
                grad_rows,
                value_blocks[block_index],
                preferred_element_type=jnp.float32,
            )
            grad_scores = (soft_weights * (grad_weights - delta_sum[..., None])).astype(
                jnp.bfloat16
            )
            grad_query = (
                grad_query
                + jnp.einsum(
                    "hqk,khd->qhd",
                    grad_scores,
                    key_blocks[block_index],
                    preferred_element_type=jnp.float32,
                )
                * scaling
            )
            key_part = (
                jnp.einsum(
                    "hqk,qhd->khd", grad_scores, query_rows, preferred_element_type=jnp.float32
                )
                * scaling
            )
            value_part = jnp.einsum(
                "hqk,qhd->khd",
                soft_weights.astype(jnp.bfloat16),
                grad_rows,
                preferred_element_type=jnp.float32,
            )
            keys_acc = keys_acc.at[block_index].add(key_part)
            values_acc = values_acc.at[block_index].add(value_part)
            table_acc = table_acc + bias_pull(grad_scores.astype(jnp.float32))[0]
            return (grad_query, keys_acc, values_acc, table_acc)

        return (lax.cond(live_at(block_index), grad_update, lambda current: current, state), None)

    start_state = (
        jnp.zeros((block_rows, head_total, head_dim), jnp.float32),
        grad_keys,
        grad_values,
        grad_table,
    )
    final_state, unused = lax.scan(grad_step, start_state, jnp.arange(block_total, dtype=jnp.int32))
    return final_state


def norm_forward(values, gain_vec):
    inverse = lax.rsqrt(jnp.mean(values * values, axis=-1, keepdims=True) + EPSILON)
    return (values * inverse * gain_vec, inverse)


def norm_backward(values, inverse, gain_vec, grad_norm):
    scaled = grad_norm * gain_vec
    inner = jnp.mean(scaled * values, axis=-1, keepdims=True)
    grad_values = inverse * scaled - values * inverse**3 * inner
    grad_gain = jnp.sum(grad_norm * values * inverse, axis=0)
    return (grad_values, grad_gain)


def local(
    tokens,
    order,
    expert_ids,
    norm1_gain,
    w_query,
    w_key,
    w_value,
    w_attn_out,
    rel_table,
    norm2_gain,
    w_router,
    w_in,
    w_out,
    cotangent,
):
    head_size_axis = lax.axis_size("head")
    head_rank = lax.axis_index("head")
    blk_rank = lax.axis_index("blk")
    group_rank = lax.axis_index("dp")
    gain_one, weight_q, weight_k, weight_v, output_weight, table_all, gain_two, router_weight = (
        lax.all_gather(norm1_gain, ("dp", "blk", "head"), axis=0, tiled=True),
        lax.all_gather(w_query, ("dp", "blk", "head"), axis=0, tiled=True),
        lax.all_gather(w_key, ("dp", "blk", "head"), axis=0, tiled=True),
        lax.all_gather(w_value, ("dp", "blk", "head"), axis=0, tiled=True),
        lax.all_gather(w_attn_out, ("dp", "blk", "head"), axis=0, tiled=True),
        lax.all_gather(rel_table, ("dp", "blk", "head"), axis=0, tiled=True),
        lax.all_gather(norm2_gain, ("dp", "blk", "head"), axis=0, tiled=True),
        lax.all_gather(w_router, ("dp", "blk", "head"), axis=0, tiled=True),
    )
    seq_count, piece_rows, model_width = tokens.shape
    token_count = seq_count * piece_rows
    local_heads = HEAD_COUNT // head_size_axis
    head_width = model_width // head_size_axis
    gain_one_f = gain_one.astype(jnp.float32)
    gain_two_f = gain_two.astype(jnp.float32)
    flat_in = tokens.astype(jnp.float32).reshape(token_count, model_width)
    normed_one, inverse_one = norm_forward(flat_in, gain_one_f)
    normed_low = normed_one.astype(jnp.bfloat16)

    def project(weight_matrix):
        return (
            jnp.dot(normed_low, weight_matrix, preferred_element_type=jnp.float32)
            .astype(jnp.bfloat16)
            .reshape(seq_count, piece_rows, model_width)
        )

    query_heads, key_heads, value_heads = (
        lax.all_to_all(project(weight_q), "head", split_axis=2, concat_axis=1, tiled=True),
        lax.all_to_all(project(weight_k), "head", split_axis=2, concat_axis=1, tiled=True),
        lax.all_to_all(project(weight_v), "head", split_axis=2, concat_axis=1, tiled=True),
    )
    key_all, value_all = (
        lax.all_gather(key_heads, "blk", axis=1, tiled=True),
        lax.all_gather(value_heads, "blk", axis=1, tiled=True),
    )
    table_heads = lax.dynamic_slice_in_dim(
        table_all.astype(jnp.float32).reshape(HEAD_COUNT, BUCKETS),
        head_rank * local_heads,
        local_heads,
        0,
    )
    span_rows = query_heads.shape[1]
    block_rows = min(512, span_rows)
    query_blocks = span_rows // block_rows
    key_block_count = key_all.shape[1] // block_rows
    query_split = query_heads.reshape(seq_count, query_blocks, block_rows, local_heads, HEAD_SIZE)
    key_split = key_all.reshape(seq_count, key_block_count, block_rows, local_heads, HEAD_SIZE)
    value_split = value_all.reshape(seq_count, key_block_count, block_rows, local_heads, HEAD_SIZE)
    first_row = blk_rank * span_rows

    def forward_sequence(inputs):
        query_seq, key_seq, value_seq = inputs

        def forward_block(block_index):
            return attend_forward(
                query_seq[block_index],
                key_seq,
                value_seq,
                table_heads,
                first_row + block_index * block_rows,
                BLOCK,
            )

        return lax.map(forward_block, jnp.arange(query_blocks, dtype=jnp.int32))

    attended_values, log_totals = lax.map(forward_sequence, (query_split, key_split, value_split))
    attended_heads = attended_values.reshape(seq_count, span_rows, head_width)
    weight_o_rows = lax.dynamic_slice_in_dim(output_weight, head_rank * head_width, head_width, 0)
    partial_out = jnp.einsum(
        "spd,de->spe", attended_heads, weight_o_rows, preferred_element_type=jnp.float32
    )
    attn_result = lax.psum_scatter(
        partial_out.astype(jnp.bfloat16), "head", scatter_dimension=1, tiled=True
    ).astype(jnp.float32)
    middle = flat_in + attn_result.reshape(token_count, model_width)
    normed_two, inverse_two = norm_forward(middle, gain_two_f)
    routed_low = normed_two.astype(jnp.bfloat16)
    router_logits = jnp.dot(routed_low, router_weight, preferred_element_type=jnp.float32)
    router_probs = jax.nn.softmax(router_logits, axis=-1)
    expert_count = router_weight.shape[1]
    columns = jnp.arange(expert_count, dtype=jnp.int32)
    total_tokens = expert_ids.shape[0] * expert_ids.shape[1]
    tallies = jnp.sum(
        (expert_ids.reshape(total_tokens, 1) == columns[None, :]).astype(jnp.float32), axis=0
    )
    piece_rank = blk_rank * head_size_axis + head_rank
    own_ids = lax.dynamic_slice(
        expert_ids, (group_rank * seq_count, piece_rank * piece_rows, 0), (seq_count, piece_rows, 1)
    ).reshape(token_count)
    chosen = own_ids[:, None] == columns[None, :]
    gate_value = jnp.sum(jnp.where(chosen, router_probs, 0.0), axis=1)
    priority = (
        order.reshape(token_count) * seq_count
        + jnp.arange(token_count, dtype=jnp.int32) // piece_rows
    )
    earlier = (priority[None, :] < priority[:, None]) & (own_ids[None, :] == own_ids[:, None])
    queue_rank = jnp.sum(earlier.astype(jnp.int32), axis=1)
    capacity = (5 * token_count + 4 * expert_count - 1) // (4 * expert_count)
    slot_index = own_ids * capacity + queue_rank
    route_table = (
        (slot_index[None, :] == jnp.arange(expert_count * capacity, dtype=jnp.int32)[:, None])
        & (queue_rank < capacity)[None, :]
    ).astype(jnp.bfloat16)
    outgoing = (
        jnp.dot(route_table, routed_low, preferred_element_type=jnp.float32)
        .astype(jnp.bfloat16)
        .reshape(expert_count, capacity, model_width)
    )
    incoming = lax.all_to_all(outgoing, ("dp", "blk"), split_axis=0, concat_axis=0, tiled=True)
    local_experts = w_in.shape[0]
    sources = expert_count // local_experts
    grouped = incoming.reshape(sources, local_experts, capacity, model_width)
    pre_act = jnp.einsum("necd,edf->necf", grouped, w_in, preferred_element_type=jnp.float32)
    hidden = jax.nn.gelu(pre_act, approximate=False).astype(jnp.bfloat16)
    expert_out = jnp.einsum(
        "necf,efd->necd", hidden, w_out, preferred_element_type=jnp.float32
    ).astype(jnp.bfloat16)
    returned = lax.all_to_all(
        expert_out.reshape(expert_count, capacity, model_width),
        ("dp", "blk"),
        split_axis=0,
        concat_axis=0,
        tiled=True,
    )
    expert_rows = jnp.einsum(
        "cs,cd->sd",
        route_table,
        returned.reshape(expert_count * capacity, model_width),
        preferred_element_type=jnp.float32,
    )
    layer_result = middle + gate_value[:, None] * expert_rows
    layer_out = layer_result.astype(jnp.bfloat16).reshape(seq_count, piece_rows, model_width)
    grad_result = cotangent.astype(jnp.float32).reshape(token_count, model_width)
    grad_gate = jnp.sum(grad_result * expert_rows, axis=1)
    grad_rows_low = (gate_value[:, None] * grad_result).astype(jnp.bfloat16)
    grad_outgoing = (
        jnp.dot(route_table, grad_rows_low, preferred_element_type=jnp.float32)
        .astype(jnp.bfloat16)
        .reshape(expert_count, capacity, model_width)
    )
    grad_expert = lax.all_to_all(
        grad_outgoing, ("dp", "blk"), split_axis=0, concat_axis=0, tiled=True
    ).reshape(sources, local_experts, capacity, model_width)
    grad_hidden = jnp.einsum(
        "necd,efd->necf", grad_expert, w_out, preferred_element_type=jnp.float32
    ).astype(jnp.bfloat16)
    grad_pre = (grad_hidden.astype(jnp.float32) * gelu_slope(pre_act)).astype(jnp.bfloat16)
    grad_w_out = jnp.einsum(
        "necf,necd->efd", hidden, grad_expert, preferred_element_type=jnp.float32
    )
    grad_w_in = jnp.einsum("necd,necf->edf", grouped, grad_pre, preferred_element_type=jnp.float32)
    grad_grouped = jnp.einsum(
        "necf,edf->necd", grad_pre, w_in, preferred_element_type=jnp.float32
    ).astype(jnp.bfloat16)
    grad_returned = lax.all_to_all(
        grad_grouped.reshape(expert_count, capacity, model_width),
        ("dp", "blk"),
        split_axis=0,
        concat_axis=0,
        tiled=True,
    )
    grad_routed = jnp.einsum(
        "cs,cd->sd",
        route_table,
        grad_returned.reshape(expert_count * capacity, model_width),
        preferred_element_type=jnp.float32,
    )
    share = AUX_WEIGHT * expert_count * tallies / total_tokens
    grad_probs = jnp.where(chosen, grad_gate[:, None], 0.0) + share[None, :]
    grad_logits = (
        router_probs * (grad_probs - jnp.sum(router_probs * grad_probs, axis=1, keepdims=True))
    ).astype(jnp.bfloat16)
    grad_router = jnp.einsum(
        "td,te->de", routed_low, grad_logits, preferred_element_type=jnp.float32
    )
    grad_routed = grad_routed + jnp.einsum(
        "te,de->td", grad_logits, router_weight, preferred_element_type=jnp.float32
    )
    grad_mid_norm, grad_gain_two = norm_backward(middle, inverse_two, gain_two_f, grad_routed)
    grad_middle = grad_result + grad_mid_norm
    grad_mid_low = grad_middle.astype(jnp.bfloat16).reshape(seq_count, piece_rows, model_width)
    grad_mid_all = lax.all_gather(grad_mid_low, "head", axis=1, tiled=True)
    grad_attended = jnp.einsum(
        "spe,de->spd", grad_mid_all, weight_o_rows, preferred_element_type=jnp.float32
    ).astype(jnp.bfloat16)
    grad_wo_rows = jnp.einsum(
        "spd,spe->de", attended_heads, grad_mid_all, preferred_element_type=jnp.float32
    )
    grad_weight_o = lax.dynamic_update_slice(
        jnp.zeros((model_width, model_width), jnp.float32),
        grad_wo_rows,
        (head_rank * head_width, 0),
    )
    grad_split = grad_attended.reshape(seq_count, query_blocks, block_rows, local_heads, HEAD_SIZE)

    def backward_sequence(inputs):
        query_seq, key_seq, value_seq, total_seq, grad_seq = inputs

        def backward_block(state, block_index):
            keys_acc, values_acc, table_acc = state
            grad_query, keys_acc, values_acc, table_acc = attend_backward(
                query_seq[block_index],
                key_seq,
                value_seq,
                table_heads,
                total_seq[block_index],
                grad_seq[block_index],
                first_row + block_index * block_rows,
                BLOCK,
                keys_acc,
                values_acc,
                table_acc,
            )
            return ((keys_acc, values_acc, table_acc), grad_query)

        start_state = (
            jnp.zeros(key_seq.shape, jnp.float32),
            jnp.zeros(value_seq.shape, jnp.float32),
            jnp.zeros(table_heads.shape, jnp.float32),
        )
        (keys_acc, values_acc, table_acc), grad_query = lax.scan(
            backward_block, start_state, jnp.arange(query_blocks, dtype=jnp.int32)
        )
        return (grad_query, keys_acc, values_acc, table_acc)

    grad_query, grad_keys, grad_values, grad_tables = lax.map(
        backward_sequence, (query_split, key_split, value_split, log_totals, grad_split)
    )
    grad_key_own, grad_value_own = (
        lax.psum_scatter(
            grad_keys.reshape(seq_count, key_block_count * block_rows, head_width).astype(
                jnp.bfloat16
            ),
            "blk",
            scatter_dimension=1,
            tiled=True,
        ).astype(jnp.float32),
        lax.psum_scatter(
            grad_values.reshape(seq_count, key_block_count * block_rows, head_width).astype(
                jnp.bfloat16
            ),
            "blk",
            scatter_dimension=1,
            tiled=True,
        ).astype(jnp.float32),
    )
    grad_q_tok, grad_k_tok, grad_v_tok = (
        lax.all_to_all(
            grad_query.reshape(seq_count, span_rows, head_width).astype(jnp.bfloat16),
            "head",
            split_axis=1,
            concat_axis=2,
            tiled=True,
        ),
        lax.all_to_all(
            grad_key_own.astype(jnp.bfloat16), "head", split_axis=1, concat_axis=2, tiled=True
        ),
        lax.all_to_all(
            grad_value_own.astype(jnp.bfloat16), "head", split_axis=1, concat_axis=2, tiled=True
        ),
    )
    grad_q_flat = grad_q_tok.reshape(token_count, model_width)
    grad_k_flat = grad_k_tok.reshape(token_count, model_width)
    grad_v_flat = grad_v_tok.reshape(token_count, model_width)
    grad_weight_q = jnp.einsum(
        "td,te->de", normed_low, grad_q_flat, preferred_element_type=jnp.float32
    )
    grad_weight_k = jnp.einsum(
        "td,te->de", normed_low, grad_k_flat, preferred_element_type=jnp.float32
    )
    grad_weight_v = jnp.einsum(
        "td,te->de", normed_low, grad_v_flat, preferred_element_type=jnp.float32
    )
    grad_normed = jnp.einsum("te,de->td", grad_q_flat, weight_q, preferred_element_type=jnp.float32)
    grad_normed = grad_normed + jnp.einsum(
        "te,de->td", grad_k_flat, weight_k, preferred_element_type=jnp.float32
    )
    grad_normed = grad_normed + jnp.einsum(
        "te,de->td", grad_v_flat, weight_v, preferred_element_type=jnp.float32
    )
    grad_in_norm, grad_gain_one = norm_backward(flat_in, inverse_one, gain_one_f, grad_normed)
    grad_tokens = (
        (grad_middle + grad_in_norm)
        .astype(jnp.bfloat16)
        .reshape(seq_count, piece_rows, model_width)
    )
    grad_table_heads = jnp.sum(grad_tables, axis=0).reshape(local_heads * BUCKETS)
    grad_table_all = lax.dynamic_update_slice(
        jnp.zeros((HEAD_COUNT * BUCKETS,), jnp.float32),
        grad_table_heads,
        (head_rank * local_heads * BUCKETS,),
    )
    owned = (
        lax.psum_scatter(grad_gain_one, ("dp", "blk", "head"), scatter_dimension=0, tiled=True),
        lax.psum_scatter(grad_weight_q, ("dp", "blk", "head"), scatter_dimension=0, tiled=True),
        lax.psum_scatter(grad_weight_k, ("dp", "blk", "head"), scatter_dimension=0, tiled=True),
        lax.psum_scatter(grad_weight_v, ("dp", "blk", "head"), scatter_dimension=0, tiled=True),
        lax.psum_scatter(grad_weight_o, ("dp", "blk", "head"), scatter_dimension=0, tiled=True),
        lax.psum_scatter(grad_table_all, ("dp", "blk", "head"), scatter_dimension=0, tiled=True),
        lax.psum_scatter(grad_gain_two, ("dp", "blk", "head"), scatter_dimension=0, tiled=True),
        lax.psum_scatter(grad_router, ("dp", "blk", "head"), scatter_dimension=0, tiled=True),
    )
    summed_in, summed_out = (
        lax.psum(grad_w_in.astype(jnp.bfloat16), "head").astype(jnp.float32),
        lax.psum(grad_w_out.astype(jnp.bfloat16), "head").astype(jnp.float32),
    )
    return (
        layer_out,
        grad_tokens,
        owned[0],
        owned[1],
        owned[2],
        owned[3],
        owned[4],
        owned[5],
        owned[6],
        owned[7],
        summed_in,
        summed_out,
    )


def solution(mesh):
    in_specs = (
        P("dp", ("blk", "head"), None),
        P("dp", ("blk", "head")),
        P(),
        P(("dp", "blk", "head")),
        P(("dp", "blk", "head"), None),
        P(("dp", "blk", "head"), None),
        P(("dp", "blk", "head"), None),
        P(("dp", "blk", "head"), None),
        P(("dp", "blk", "head")),
        P(("dp", "blk", "head")),
        P(("dp", "blk", "head"), None),
        P(("dp", "blk"), None, None),
        P(("dp", "blk"), None, None),
        P("dp", ("blk", "head"), None),
    )
    out_specs = (
        P("dp", ("blk", "head"), None),
        P("dp", ("blk", "head"), None),
        P(("dp", "blk", "head")),
        P(("dp", "blk", "head"), None),
        P(("dp", "blk", "head"), None),
        P(("dp", "blk", "head"), None),
        P(("dp", "blk", "head"), None),
        P(("dp", "blk", "head")),
        P(("dp", "blk", "head")),
        P(("dp", "blk", "head"), None),
        P(("dp", "blk"), None, None),
        P(("dp", "blk"), None, None),
    )
    return jax.shard_map(local, mesh=mesh, in_specs=in_specs, out_specs=out_specs, check_vma=False)
```

profile of v0, /device:TPU:0, one launch (start us, length us, event | category | flops | bytes accessed | tf_op | source)
XLA Modules:
  0.0 1858.5 jit_solution(5209178891120768430)
XLA Ops:
  12.5 42.1 %all-reduce.10 = (bf16[768]{0:T(1024)(128)(2,1)S(1)}, bf16[384]{0:T(512)(128)(2,1)S(1)}, bf16[768]{0:T(1024)(128)(2,1)}) all-reduce(bf16[768]{0:T(1024)(128)(2,1)S(1)} %dynamic-update-slice.6, bf16[384]{0:T(512)(128)(2,1)S(1)} %dynamic-update-slice.7, ...), channel_id=1, replica_groups=mesh['dp'=2,'blk'=4,'head'=4] {'dp','blk','head'}, use_global_device_ids=true, to_apply=%add.2 | all-reduce | flops 1920 | bytes 7680
  57.0 10.8 all-gather.9.cloned.1.call-done
  76.4 47.4 %all-gather.11.cloned.1.call-done = bf16[768,768]{1,0:T(8,128)(2,1)} async-done(((bf16[24,768]{1,0:T(8,128)(2,1)}), bf16[768,768]{1,0:T(8,128)(2,1)}) %all-gather.11.cloned.1.call-update) | async-done | bytes 1179664 | tf_op jit(solution)/shard_map/all_gather | solution.py:281
  128.3 3.4 all-to-all-start.2
  131.7 48.0 %all-gather.7.cloned.1.call-done = bf16[768,768]{1,0:T(8,128)(2,1)} async-done(((bf16[24,768]{1,0:T(8,128)(2,1)}), bf16[768,768]{1,0:T(8,128)(2,1)}) %all-gather.7.cloned.1.call-update) | async-done | bytes 1179664 | tf_op jit(solution)/shard_map/all_gather | solution.py:283
  184.5 3.4 all-to-all-start
  188.0 18.9 %all_gather.37 = bf16[1,2048,192]{1,2,0:T(8,128)(2,1)S(1)} all-gather(bf16[1,512,192]{1,2,0:T(8,128)(2,1)S(1)} %bitcast.457), channel_id=1, replica_groups=mesh['dp'=2,'blk'=4,'head'=4] {'blk'}, dimensions={1}, use_global_device_ids=true | all-gather | bytes 983040 | tf_op jit(solution)/shard_map/all_gather | solution.py:312
  209.2 19.1 %all_gather.35 = bf16[1,2048,192]{1,2,0:T(8,128)(2,1)S(1)} all-gather(bf16[1,512,192]{1,2,0:T(8,128)(2,1)S(1)} %bitcast.458), channel_id=1, replica_groups=mesh['dp'=2,'blk'=4,'head'=4] {'blk'}, dimensions={1}, use_global_device_ids=true | all-gather | bytes 983040 | tf_op jit(solution)/shard_map/all_gather | solution.py:313
  230.0 44.9 %while.128 = (s32[]{:T(128)}, f32[3,512]{1,0:T(4,128)S(1)}, f32[3,512]{1,0:T(4,128)S(1)}, s32[4]{0:T(128)S(1)}, s32[]{:T(128)}, /*index=5*/s32[]{:T(128)}, bf16[...) while((s32[]{:T(128)}, f32[3,512]{1,0:T(4,128)S(1)}, ...), condition=%wide.region_6.7_spmd, body=%wide.region_1.6_spmd.sunk | while | flops 106929176 | bytes 70220688 | solution.py:99
  231.4 39.2 %conditional.8 = ((f32[3,512]{1,0:T(4,128)S(1)}, f32[3,512]{1,0:T(4,128)S(1)})) conditional(s32[]{:T(128)} %convert_element_type.897, (f32[3,512]{1,0:T(4,128)S(1)}, f32[3,512]{1,0:T(4,128)S(1)}) %tuple.187, (s32[]{:T(128)}, s32[]{:T(128)}, bf16[4,512,3,64]{1,3,2,0:T(8,128)(2,1)}, bf16[512,3,64]{0,2,1:T(8,128)(2,1)S(1)}, f32[3,32]{1,0:T(4,128)}, ...), branch_computations={%region_2.2_spmd, %region_3.5_spmd} | conditional | flops 106929160 | bytes 70220280 | solution.py:93
  232.9 3.5 broadcast_bitcast_fusion
  236.4 7.1 copy.224
  243.5 4.1 slice.72
  247.6 13.2 reshape.1078
  275.7 45.4 %while.129 = (s32[]{:T(128)}, f32[512,3,64]{0,2,1:T(8,128)}, s32[4]{0:T(128)S(1)}, s32[]{:T(128)}, bf16[4,512,3,64]{1,3,2,0:T(8,128)(2,1)}, /*index=5*/s32[]{:T(...) while((s32[]{:T(128)}, f32[512,3,64]{0,2,1:T(8,128)}, ...), condition=%wide.region_10.11_spmd, body=%wide.region_7.10_spmd.sunk | while | flops 206901264 | bytes 64839548 | solution.py:122
  277.0 40.1 %conditional.9 = (f32[512,3,64]{0,2,1:T(8,128)}) conditional(s32[]{:T(128)} %convert_element_type.898, f32[512,3,64]{0,2,1:T(8,128)} %get-tuple-element.1676, (s32[]{:T(128)}, bf16[4,512,3,64]{1,3,2,0:T(8,128)(2,1)}, s32[]{:T(128)}, bf16[4,512,3,64]{1,3,2,0:T(8,128)(2,1)}, bf16[512,3,64]{0,2,1:T(8,128)(2,1)S(1)}, /*index=5*/f32[3,32]{1,0:T(4,128)}, ...), branch_computations={%region_8.8_spmd, %region_9.9_spmd} | conditional | flops 206901248 | bytes 64839140 | solution.py:118
  278.5 3.5 broadcast_bitcast_fusion.1
  282.0 7.1 copy.225
  289.1 4.1 slice.74
  293.2 13.2 reshape.1080
  312.8 4.3 fusion.35
  325.0 260.3 %reduce-scatter.9.cloned.1.call-done = bf16[1,128,768]{2,1,0:T(8,128)(2,1)} async-done(((bf16[1,512,768]{2,1,0:T(8,128)(2,1)}), bf16[1,128,768]{2,1,0:T(8,128)(2,1)}) %reduce-scatter.9.cloned.1.call-update) | async-done | bytes 196624 | tf_op jit(solution)/shard_map/reduce_scatter | solution.py:351
  588.4 5.5 all-to-all-start.3
  594.0 10.3 all-to-all-done.3
  604.4 8.5 fusion.199
  612.9 4.7 fusion.215
  617.5 3.4 all-to-all-start.4
  621.0 41.1 %all-gather.1 = bf16[32,24,8]{1,2,0:T(8,128)(2,1)S(1)} all-gather(bf16[1,24,8]{1,2,0:T(8,128)(2,1)S(1)} %bitcast.460), channel_id=1, replica_groups=mesh['dp'=2,'blk'=4,'head'=4] {'dp','blk','head'}, dimensions={0}, use_global_device_ids=true | all-gather | bytes 12672 | tf_op jit(solution)/shard_map/all_gather | solution.py:287
  664.1 13.6 all_to_all.116
  677.7 5.9 fusion.194
  683.7 5.2 fusion.212
  688.9 3.4 all-to-all-start.6
  692.8 9.9 all-to-all-done.6
  703.8 7.2 all-gather
  713.8 47.3 %while.130 = (s32[]{:T(128)}, f32[3,512]{1,0:T(4,128)S(1)}, s32[4]{0:T(128)}, s32[]{:T(128)}, s32[]{:T(128)}, /*index=5*/bf16[4,512,3,64]{1,3,2,0:T(8,128)(2,1)}...) while((s32[]{:T(128)}, f32[3,512]{1,0:T(4,128)S(1)}, ...), condition=%wide.region_25.26_spmd, body=%wide.region_21.25_spmd.sunk | while | flops 207589392 | bytes 83147696 | solution.py:182
  716.0 39.6 %conditional.10 = (f32[3,512]{1,0:T(4,128)S(1)}) conditional(s32[]{:T(128)} %convert_element_type.899, f32[3,512]{1,0:T(4,128)S(1)} %get-tuple-element.1725, (s32[]{:T(128)}, s32[]{:T(128)}, bf16[4,512,3,64]{1,3,2,0:T(8,128)(2,1)}, bf16[512,3,64]{0,2,1:T(8,128)(2,1)S(1)}, f32[3,32]{1,0:T(4,128)}, /*index=5*/f32[1,3,512]{2,1,0:T(4,128)S(1)}, ...), branch_computations={%region_22.22_spmd, %region_23.24_spmd} | conditional | flops 207589376 | bytes 83147272 | solution.py:178
  717.4 3.5 broadcast_bitcast_fusion.2
  720.9 7.1 copy.226
  728.0 4.1 slice.76
  732.1 13.2 reshape.1082
  763.8 107.7 %while.131 = (s32[]{:T(128)}, f32[512,3,64]{0,2,1:T(8,128)S(1)}, f32[4,512,3,64]{1,3,2,0:T(8,128)S(1)}, f32[4,512,3,64]{1,3,2,0:T(8,128)}, f32[3,32]{1,0:T(4,128...) while((s32[]{:T(128)}, f32[512,3,64]{0,2,1:T(8,128)S(1)}, ...), condition=%wide.region_31.32_spmd, body=%wide.region_26.31_spmd.sunk | while | flops 516195488 | bytes 136457840 | solution.py:242
  783.6 73.6 %conditional.11 = ((f32[512,3,64]{0,2,1:T(8,128)S(1)}, f32[4,512,3,64]{1,3,2,0:T(8,128)S(1)}, f32[4,512,3,64]{1,3,2,0:T(8,128)}, f32[3,32]{1,0:T(4,128)})) conditional(s32[]{:T(128)} %convert_element_type.900, (f32[512,3,64]{0,2,1:T(8,128)S(1)}, f32[4,512,3,64]{1,3,2,0:T(8,128)S(1)}, f32[4,512,3,64]{1,3,2,0:T(8,128)}, ...), branch_computations={%region_27.27_spmd, %region_28.30_spmd} | conditional | flops 516195456 | bytes 136457312 | solution.py:234
  785.2 3.5 broadcast_bitcast_fusion.3
  788.7 7.1 copy.227
  795.8 4.1 slice.78
  799.8 13.2 reshape.1084
  835.5 7.4 reshape.1172
  842.9 5.6 reshape.1087
  848.5 3.9 pad_convert_fusion
  876.1 5.0 fusion.174
  881.1 3.6 fusion.175
  890.9 8.3 all_to_all.117
  902.1 331.7 %reduce-scatter.11.cloned.1.call-done = bf16[1,512,192]{1,2,0:T(8,128)(2,1)} async-done(((bf16[1,2048,192]{1,2,0:T(8,128)(2,1)}), bf16[1,512,192]{1,2,0:T(8,128)(2,1)}) %reduce-scatter.11.cloned.1.call-update) | async-done | bytes 196624 | tf_op jit(solution)/shard_map/reduce_scatter | solution.py:509
  1237.6 8.1 all_to_all.118
  1248.6 10.2 reduce-scatter.13.cloned.1.call-done
  1262.6 10.0 all_to_all.119
  1281.2 38.5 %all-reduce.9 = (f32[768]{0:T(1024)S(1)}, f32[384]{0:T(512)S(1)}, f32[768]{0:T(1024)S(1)}, f32[768,8]{0,1:T(8,128)S(1)}) all-reduce(f32[768]{0:T(1024)S(1)} %get-tuple-element.1189, f32[384]{0:T(512)S(1)} %copy-done.53, f32[768]{0:T(1024)S(1)} %copy-done.46, ...), channel_id=6, replica_groups=mesh['dp'=2,'blk'=4,'head'=4] {'dp','blk','head'}, use_global_device_ids=true, to_apply=%region_36.37.clone | all-reduce | flops 8064 | bytes 64512
  1323.3 109.7 %all-reduce.14.cloned.1.call-done = (bf16[1,768,3072]{2,1,0:T(8,128)(2,1)}, bf16[1,3072,768]{2,1,0:T(8,128)(2,1)}) async-done(((bf16[1,768,3072]{2,1,0:T(8,128)(2,1)}, bf16[1,3072,768]{2,1,0:T(8,128)(2,1)}), (bf16[1,768,3072]{2,1,0:T(8,128)(2,1)}, bf16[1,3072,768]{2,1,0:T(8,128)(2,1)})) %all-reduce.14.cloned.1.call-update) | async-done | bytes 9437200 | tf_op jit(solution)/shard_map/psum | solution.py:583
  1433.0 7.5 convert_element_type.679
  1440.6 4.5 convert_element_type.682
  1445.0 93.9 %reduce-scatter.21.cloned.1.call-done = f32[24,768]{1,0:T(8,128)} async-done(((f32[768,768]{1,0:T(8,128)}), f32[24,768]{1,0:T(8,128)}) %reduce-scatter.21.cloned.1.call-update) | async-done | bytes 73744 | tf_op jit(solution)/shard_map/reduce_scatter | solution.py:577
  1539.0 103.8 %reduce-scatter.15.cloned.1.call-done = f32[24,768]{1,0:T(8,128)} async-done(((f32[768,768]{1,0:T(8,128)}), f32[24,768]{1,0:T(8,128)}) %reduce-scatter.15.cloned.1.call-update) | async-done | bytes 73744 | tf_op jit(solution)/shard_map/reduce_scatter | solution.py:574
  1642.8 104.8 %reduce-scatter.17.cloned.1.call-done = f32[24,768]{1,0:T(8,128)} async-done(((f32[768,768]{1,0:T(8,128)}), f32[24,768]{1,0:T(8,128)}) %reduce-scatter.17.cloned.1.call-update) | async-done | bytes 73744 | tf_op jit(solution)/shard_map/reduce_scatter | solution.py:575
  1747.6 103.8 %reduce-scatter.19.cloned.1.call-done = f32[24,768]{1,0:T(8,128)} async-done(((f32[768,768]{1,0:T(8,128)}), f32[24,768]{1,0:T(8,128)}) %reduce-scatter.19.cloned.1.call-update) | async-done | bytes 73744 | tf_op jit(solution)/shard_map/reduce_scatter | solution.py:576
  (386 shorter events, 145.5 us)
Async XLA Ops:
  7.2 116.6 %copy-start.1 = (bf16[1,128,768]{2,1,0:T(8,128)(2,1)S(1)}, bf16[1,128,768]{2,1,0:T(8,128)(2,1)}, u32[]{:S(2)}) copy-start(bf16[1,128,768]{2,1,0:T(8,128)(2,1)} %param.34) | copy-start | bytes 589828
  7.2 60.6 %all-gather.9.cloned.1.call-start = ((), (), s32[]{:S(2)}) async-start(), calls=%async_computation.18 | async-start | bytes 1216512 | tf_op jit(solution)/shard_map/all_gather | solution.py:282
  7.9 115.8 %all-gather.11.cloned.1.call-start = ((), (), s32[]{:S(2)}) async-start(), calls=%async_computation.19 | async-start | bytes 1216512 | tf_op jit(solution)/shard_map/all_gather | solution.py:281
  8.7 171.0 %all-gather.7.cloned.1.call-start = ((), (), s32[]{:S(2)}) async-start(), calls=%async_computation.17 | async-start | bytes 1216512 | tf_op jit(solution)/shard_map/all_gather | solution.py:283
  9.4 312.9 %all-gather.13.cloned.1.call-start = ((), (), s32[]{:S(2)}) async-start(), calls=%async_computation.20 | async-start | bytes 1216512 | tf_op jit(solution)/shard_map/all_gather | solution.py:284
  54.7 125.0 %copy-start.30 = (f32[768]{0:T(1024)}, f32[768]{0:T(1024)S(1)}, u32[]{:S(2)}) copy-start(f32[768]{0:T(1024)S(1)} %convert_element_type.640) | copy-start | bytes 9220
  57.0 122.7 %copy-start.42 = (f32[128]{0:T(128)}, f32[128]{0:T(128)S(1)}, u32[]{:S(2)}) copy-start(f32[128]{0:T(128)S(1)} %get-tuple-element.1305) | copy-start | bytes 1540
  73.0 55.3 %all-to-all-start.1 = ((bf16[4,2,12288]{2,1,0:T(2,128)(2,1)}), bf16[4,2,12288]{2,1,0:T(2,128)(2,1)S(1)}, u32[]{:S(2)}, u32[]{:S(2)}) async-start(bf16[4,2,12288]{2,1,0:T(2,128)(2,1)} %reshape.1176), calls=%async_computation.1 | async-start | bytes 393216 | tf_op jit(solution)/shard_map/all_to_all | solution.py:308
  128.3 56.2 %all-to-all-start.2 = ((bf16[4,2,12288]{2,1,0:T(2,128)(2,1)}), bf16[4,2,12288]{2,1,0:T(2,128)(2,1)S(1)}, u32[]{:S(2)}, u32[]{:S(2)}) async-start(bf16[4,2,12288]{2,1,0:T(2,128)(2,1)} %reshape.1178), calls=%async_computation.2 | async-start | bytes 393216 | tf_op jit(solution)/shard_map/all_to_all | solution.py:307
  184.5 24.4 %all-to-all-start = ((bf16[4,2,12288]{2,1,0:T(2,128)(2,1)}), bf16[4,2,12288]{2,1,0:T(2,128)(2,1)S(1)}, u32[]{:S(2)}, u32[]{:S(2)}) async-start(bf16[4,2,12288]{2,1,0:T(2,128)(2,1)} %reshape.1174), calls=%async_computation | async-start | bytes 393216 | tf_op jit(solution)/shard_map/all_to_all | solution.py:309
  187.9 397.3 %reduce-scatter.9.cloned.1.call-start = ((), (), s32[]{:S(2)}) async-start(), calls=%async_computation.21 | async-start | bytes 983040 | tf_op jit(solution)/shard_map/reduce_scatter | solution.py:351
  321.2 264.1 %copy-start.2 = (bf16[1,128,768]{2,1,0:T(8,128)(2,1)S(1)}, bf16[1,128,768]{2,1,0:T(8,128)(2,1)}, u32[]{:S(2)}) copy-start(bf16[1,128,768]{2,1,0:T(8,128)(2,1)} %param.34) | copy-start | bytes 589828
  322.3 264.1 %copy-start.27 = (bf16[512,3,64]{0,2,1:T(8,128)(2,1)}, bf16[512,3,64]{0,2,1:T(8,128)(2,1)S(1)}, u32[]{:S(2)}) copy-start(bf16[512,3,64]{0,2,1:T(8,128)(2,1)S(1)} %convert_element_type.645) | copy-start | bytes 589828
  324.6 379.0 %copy-start.38 = (f32[768]{0:T(1024)}, f32[768]{0:T(1024)S(1)}, u32[]{:S(2)}) copy-start(f32[768]{0:T(1024)S(1)} %convert_element_type.648) | copy-start | bytes 9220
  324.7 367.7 %copy-start.47 = (s32[128]{0:T(128)}, s32[128]{0:T(128)S(1)}, u32[]{:S(2)}) copy-start(s32[128]{0:T(128)S(1)} %fusion.269) | copy-start | bytes 1540
  586.3 117.3 %copy-start.54 = (f32[128]{0:T(128)}, f32[128]{0:T(128)S(1)}, u32[]{:S(2)}) copy-start(f32[128]{0:T(128)S(1)} %get-tuple-element.1307) | copy-start | bytes 1540
  586.3 117.3 %copy-start.68 = (f32[128]{0:T(128)}, f32[128]{0:T(128)S(1)}, u32[]{:S(2)}) copy-start(f32[128]{0:T(128)S(1)} %get-tuple-element.1306) | copy-start | bytes 1540
  587.4 74.9 %copy-start.25 = (bf16[128,768]{1,0:T(8,128)(2,1)}, bf16[128,768]{1,0:T(8,128)(2,1)S(1)}, u32[]{:S(2)}) copy-start(bf16[128,768]{1,0:T(8,128)(2,1)S(1)} %multiply_convert_fusion) | copy-start | bytes 589828
  588.4 16.0 all-to-all-start.3
  604.4 8.5 copy-start.32
  612.8 4.7 copy-start.74
  612.8 8.1 copy-start.66
  612.9 49.7 %copy-start.21 = (bf16[1,128,768]{2,1,0:T(8,128)(2,1)S(1)}, bf16[1,128,768]{2,1,0:T(8,128)(2,1)}, u32[]{:S(2)}) copy-start(bf16[1,128,768]{2,1,0:T(8,128)(2,1)} %param.47) | copy-start | bytes 589828
  617.5 45.0 %all-to-all-start.4 = ((bf16[8,20,768]{2,1,0:T(8,128)(2,1)}), bf16[8,20,768]{2,1,0:T(8,128)(2,1)S(1)}, u32[]{:S(2)}, u32[]{:S(2)}) async-start(bf16[8,20,768]{2,1,0:T(8,128)(2,1)} %fusion.215), calls=%async_computation.5 | async-start | bytes 589824 | tf_op jit(solution)/shard_map/all_to_all | solution.py:397
  621.0 71.4 %copy-start.62 = (f32[8]{0:T(128)}, f32[8]{0:T(128)S(1)}, u32[]{:S(2)}) copy-start(f32[8]{0:T(128)S(1)} %broadcast_multiply_fusion) | copy-start | bytes 100
  662.4 30.0 %copy-start.40 = (f32[128,8]{0,1:T(8,128)}, f32[128,8]{0,1:T(8,128)S(1)}, u32[]{:S(2)}) copy-start(f32[128,8]{0,1:T(8,128)S(1)} %get-tuple-element.1313) | copy-start | bytes 12292
  662.4 29.9 %copy-start.50 = (f32[128]{0:T(128)}, f32[128]{0:T(128)S(1)}, u32[]{:S(2)}) copy-start(f32[128]{0:T(128)S(1)} %get-tuple-element.1312) | copy-start | bytes 1540
  662.5 29.9 %copy-start.56 = (f32[128]{0:T(128)}, f32[128]{0:T(128)S(1)}, u32[]{:S(2)}) copy-start(f32[128]{0:T(128)S(1)} %fusion.266) | copy-start | bytes 1540
  663.6 28.8 %copy-start.58 = (f32[128]{0:T(128)}, f32[128]{0:T(128)S(1)}, u32[]{:S(2)}) copy-start(f32[128]{0:T(128)S(1)} %get-tuple-element.1310) | copy-start | bytes 1540
  663.7 20.0 %copy-start.60 = (f32[128]{0:T(128)}, f32[128]{0:T(128)S(1)}, u32[]{:S(2)}) copy-start(f32[128]{0:T(128)S(1)} %get-tuple-element.1192) | copy-start | bytes 1540
  663.7 28.7 %copy-start.64 = (f32[128]{0:T(128)}, f32[128]{0:T(128)S(1)}, u32[]{:S(2)}) copy-start(f32[128]{0:T(128)S(1)} %get-tuple-element.1191) | copy-start | bytes 1540
  677.7 6.0 copy-start.34
  683.7 5.2 copy-start.76
  683.7 19.0 %copy-start.14 = (bf16[1,128,768]{2,1,0:T(8,128)(2,1)S(1)}, bf16[1,128,768]{2,1,0:T(8,128)(2,1)}, u32[]{:S(2)}) copy-start(bf16[1,128,768]{2,1,0:T(8,128)(2,1)} %reduce-scatter.9.cloned.1.call-done) | copy-start | bytes 589828
  688.9 13.8 all-to-all-start.6
  692.3 541.4 %reduce-scatter.11.cloned.1.call-start = ((), (), s32[]{:S(2)}) async-start(), calls=%async_computation.22 | async-start | bytes 983040 | tf_op jit(solution)/shard_map/reduce_scatter | solution.py:509
  703.6 10.2 copy-start.19
  703.6 10.2 copy-start.70
  825.4 6.7 copy-start.6
  852.5 4.7 copy-start.7
  852.5 4.7 copy-start.9
  873.7 385.0 %reduce-scatter.13.cloned.1.call-start = ((), (), s32[]{:S(2)}) async-start(), calls=%async_computation.23 | async-start | bytes 983040 | tf_op jit(solution)/shard_map/reduce_scatter | solution.py:517
  876.0 5.1 copy-start.35
  876.0 5.1 copy-start.75
  876.1 557.0 %all-reduce.14.cloned.1.call-start = ((), (), s32[]{:S(2)}) async-start(), calls=%async_computation.28 | async-start | bytes 18874368 | tf_op jit(solution)/shard_map/psum | solution.py:583
  884.8 654.2 %reduce-scatter.21.cloned.1.call-start = ((), (), s32[]{:S(2)}) async-start(), calls=%async_computation.27 | async-start | bytes 2433024 | tf_op jit(solution)/shard_map/reduce_scatter | solution.py:577
  887.7 755.1 %reduce-scatter.15.cloned.1.call-start = ((), (), s32[]{:S(2)}) async-start(), calls=%async_computation.24 | async-start | bytes 2433024 | tf_op jit(solution)/shard_map/reduce_scatter | solution.py:574
  887.8 12.2 copy-start.3
  887.8 12.2 copy-start.31
  887.8 12.2 copy-start.43
  902.0 845.6 %reduce-scatter.17.cloned.1.call-start = ((), (), s32[]{:S(2)}) async-start(), calls=%async_computation.25 | async-start | bytes 2433024 | tf_op jit(solution)/shard_map/reduce_scatter | solution.py:575
  1248.5 602.9 %reduce-scatter.19.cloned.1.call-start = ((), (), s32[]{:S(2)}) async-start(), calls=%async_computation.26 | async-start | bytes 2433024 | tf_op jit(solution)/shard_map/reduce_scatter | solution.py:576
  1275.5 4.9 copy-start.18
  1279.9 42.3 %copy-start.15 = (bf16[1,128,768]{2,1,0:T(8,128)(2,1)S(1)}, bf16[1,128,768]{2,1,0:T(8,128)(2,1)}, u32[]{:S(2)}) copy-start(bf16[1,128,768]{2,1,0:T(8,128)(2,1)} %reduce-scatter.9.cloned.1.call-done) | copy-start | bytes 589828
  1279.9 42.3 %copy-start.20 = (f32[128,768]{1,0:T(8,128)S(1)}, f32[128,768]{1,0:T(8,128)}, u32[]{:S(2)}) copy-start(f32[128,768]{1,0:T(8,128)} %copy-done.19) | copy-start | bytes 1179652
  1279.9 42.3 %copy-start.22 = (bf16[1,128,768]{2,1,0:T(8,128)(2,1)S(1)}, bf16[1,128,768]{2,1,0:T(8,128)(2,1)}, u32[]{:S(2)}) copy-start(bf16[1,128,768]{2,1,0:T(8,128)(2,1)} %param.47) | copy-start | bytes 589828
  1279.9 42.3 %copy-start.39 = (f32[768]{0:T(1024)S(1)}, f32[768]{0:T(1024)}, u32[]{:S(2)}) copy-start(f32[768]{0:T(1024)} %copy-done.38) | copy-start | bytes 9220
  1280.5 41.7 %copy-start.29 = (f32[128,768]{1,0:T(8,128)S(1)}, f32[128,768]{1,0:T(8,128)}, u32[]{:S(2)}) copy-start(f32[128,768]{1,0:T(8,128)} %get-tuple-element.1311) | copy-start | bytes 1179652
  1280.5 41.7 %copy-start.55 = (f32[128]{0:T(128)S(1)}, f32[128]{0:T(128)}, u32[]{:S(2)}) copy-start(f32[128]{0:T(128)} %copy-done.54) | copy-start | bytes 1540
  1280.5 41.7 %copy-start.61 = (f32[128]{0:T(128)S(1)}, f32[128]{0:T(128)}, u32[]{:S(2)}) copy-start(f32[128]{0:T(128)} %copy-done.60) | copy-start | bytes 1540
  1280.5 41.7 %copy-start.69 = (f32[128]{0:T(128)S(1)}, f32[128]{0:T(128)}, u32[]{:S(2)}) copy-start(f32[128]{0:T(128)} %copy-done.68) | copy-start | bytes 1540
  1280.5 41.7 %copy-start.71 = (f32[128]{0:T(128)S(1)}, f32[128]{0:T(128)}, u32[]{:S(2)}) copy-start(f32[128]{0:T(128)} %copy-done.70) | copy-start | bytes 1540
  1280.5 41.7 %copy-start.72 = (f32[128]{0:T(128)S(1)}, f32[128]{0:T(128)}, u32[]{:S(2)}) copy-start(f32[128]{0:T(128)} %get-tuple-element.1304) | copy-start | bytes 1540
  1433.0 7.5 copy-start.16
  (35 other events, 70.5 us)
Sparse Core Ops, SparseCore 0:
  10.9 56.8 all-gather.8
  70.7 52.9 all-gather.10
  126.7 52.9 all-gather.6
  182.4 53.8 all-gather.12
  324.7 260.4 reduce-scatter.8
  873.9 359.8 reduce-scatter.10
  1236.1 22.5 reduce-scatter.12
  1262.1 170.9 all-reduce.13
  1439.8 99.1 reduce-scatter.20
  1544.7 98.0 reduce-scatter.14
  1649.5 98.0 reduce-scatter.16
  1753.3 98.0 reduce-scatter.18
where the time goes:
time: 1870 us; the launch traced here: 1860 us
  waiting for transfers between devices  1250 us (67%)
  blocking collectives  207 us (11%)
  local copies, waits for them, and re-layouts  194 us (10%)
  matrix products  82.2 us (4%)
  loops' own time  48.8 us (3%)
  other arithmetic  40.3 us (2%)
  starting transfers between devices  23 us (1%)
    reduce_scatter x1, waiting for transfers between devices, local(): lax.psum_scatter(grad_keys.reshape(seq_count, key_block_count * block_row...  332 us
    reduce_scatter x1, waiting for transfers between devices, local(): lax.psum_scatter(partial_out.astype(jnp.bfloat16), 'head', scatter_dimens...  260 us
    psum x1, waiting for transfers between devices, local(): lax.psum(grad_w_in.astype(jnp.bfloat16), 'head').astype(jnp.float32)  110 us
    reduce_scatter x1, waiting for transfers between devices, local(): lax.psum_scatter(grad_weight_k, ('dp', 'blk', 'head'), scatter_dimension=...  105 us
    reduce_scatter x1, waiting for transfers between devices, local(): lax.psum_scatter(grad_weight_q, ('dp', 'blk', 'head'), scatter_dimension=...  104 us
    reduce_scatter x1, waiting for transfers between devices, local(): lax.psum_scatter(grad_weight_v, ('dp', 'blk', 'head'), scatter_dimension=...  104 us
    reduce_scatter x1, waiting for transfers between devices, local(): lax.psum_scatter(grad_weight_o, ('dp', 'blk', 'head'), scatter_dimension=...  93.9 us
    unnamed x2, blocking collectives  80.6 us
  transfers between devices with their start and end apart: 18, of which 13 were waited for; matrix products, arithmetic and copies ran while one was open for 8% of the time, Pallas kernels for 0%

commit v1 on v0

v1 whole, which is shorter than its diff:
```python
import functools

import jax
import jax.numpy as jnp
import numpy as np
from jax import lax
from jax.experimental import pallas as pl
from jax.experimental.pallas import tpu as pltpu
from jax.sharding import PartitionSpec as P

HEAD_COUNT = 12
HEAD_SIZE = 64
BUCKETS = 32
BLOCK = 256
EPSILON = 1e-06
AUX_WEIGHT = 1.0
LIMITS = (1, 2, 3, 4, 5, 6, 7, 8, 12, 16, 23, 32, 46, 64, 91)
INV_ROOT_TWO = 0.7071067811865476
INV_ROOT_TWO_PI = 0.3989422804014327
LANES = 128
MESH = pl.DeviceIdType.MESH
F32 = jnp.float32
BF16 = jnp.bfloat16


class Sizes:
    def __init__(self, n_dp, n_blk, n_head, rows, width, experts, hidden, piece):
        self.n_dp, self.n_blk, self.n_head = n_dp, n_blk, n_head
        self.ndev = n_dp * n_blk * n_head
        self.ns = n_blk * n_head
        self.R, self.D, self.E, self.FF, self.PT = rows, width, experts, hidden, piece
        self.S = piece * self.ns
        self.nq = self.S // BLOCK
        self.hb = HEAD_COUNT // n_blk
        self.cap = (5 * piece + 4 * experts - 1) // (4 * experts)
        self.cap8 = (self.cap + 7) // 8 * 8
        self.SB = 2 * self.cap8
        self.NG = n_dp * n_blk
        self.RL = HEAD_COUNT * BUCKETS // self.ndev
        assert self.hb <= n_head and self.hb * n_blk == HEAD_COUNT
        assert experts == self.NG and n_head == 4


def nt(a, b):
    return lax.dot_general(a, b, (((1,), (1,)), ((), ())), preferred_element_type=F32)


def tn(a, b):
    return lax.dot_general(a, b, (((0,), (0,)), ((), ())), preferred_element_type=F32)


def nn(a, b):
    return jnp.dot(a, b, preferred_element_type=F32)


def place():
    return lax.axis_index("dp"), lax.axis_index("blk"), lax.axis_index("head")


def signal(device):
    pl.semaphore_signal(
        pltpu.get_barrier_semaphore(), inc=1, device_id=device, device_id_type=MESH
    )


def await_barrier(count):
    pl.semaphore_wait(pltpu.get_barrier_semaphore(), count)


def remote(src, dst, send, recv, device):
    return pltpu.make_async_remote_copy(
        src_ref=src, dst_ref=dst, send_sem=send, recv_sem=recv, device_id=device, device_id_type=MESH
    )


def flatten_rows(blocks):
    count, rows, lanes = blocks.shape
    wide = blocks.astype(F32)
    if rows % 8 == 0:
        return wide.reshape(count * rows, lanes)
    return jnp.concatenate([wide[i] for i in range(count)], axis=0)


def split_rows(dst_ref, values, rows):
    count = values.shape[0] // rows
    if rows % 8 == 0:
        dst_ref[...] = values.reshape(count, rows, values.shape[1]).astype(dst_ref.dtype)
    else:
        for i in range(count):
            dst_ref[i] = values[i * rows : (i + 1) * rows].astype(dst_ref.dtype)


def normal_parts(v):
    bell = jnp.exp(-0.5 * v * v)
    t = 1.0 / (1.0 + (0.3275911 * INV_ROOT_TWO) * jnp.abs(v))
    poly = t * (
        0.254829592
        + t * (-0.284496736 + t * (1.421413741 + t * (-1.453152027 + t * 1.061405429)))
    )
    tail = 0.5 * poly * bell
    return jnp.where(v >= 0, 1.0 - tail, tail), bell


def gather_kernel(z, x_ref, w_ref, xg_ref, wg_ref, xs, xr, ws, wr, loc):
    d, b, h = place()
    nb, nh, nd = z.n_blk, z.n_head, z.n_dp
    hy = lax.rem(h + 2, nh)
    hc = h + 1 - 2 * lax.rem(h, 2)
    hyc = lax.rem(hc + 2, nh)
    zpeers = [lax.rem(b + k, nb) for k in range(1, nb)]
    zfrom = [lax.rem(b + nb - k, nb) for k in range(1, nb)]
    dpeers = [lax.rem(d + k, nd) for k in range(1, nd)]
    dfrom = [lax.rem(d + nd - k, nd) for k in range(1, nd)]
    for p in zpeers:
        signal((d, p, h))
    signal((d, b, hy))
    signal((d, b, hc))
    for p in dpeers:
        signal((p, b, h))

    def xslot(bb, hh):
        return bb * nh + hh

    def wslot(dd, bb, hh):
        return (dd * nb + bb) * nh + hh

    own_x = xslot(b, h)
    own_w = wslot(d, b, h)
    cx = pltpu.make_async_copy(x_ref, xg_ref.at[own_x], loc.at[0])
    cw = pltpu.make_async_copy(w_ref, wg_ref.at[own_w], loc.at[1])
    cx.start()
    cw.start()
    await_barrier(nb - 1 + 2 + nd - 1)
    sent = []

    def send_x(src, slot, device):
        c = remote(src, xg_ref.at[slot], xs.at[len(sent_x)], xr.at[slot], device)
        sent_x.append(c)
        c.start()

    def send_w(src, slot, device):
        c = remote(src, wg_ref.at[slot], ws.at[len(sent_w)], wr.at[slot], device)
        sent_w.append(c)
        c.start()

    sent_x, sent_w = [], []

    def got_x(slot):
        remote(xg_ref.at[slot], xg_ref.at[slot], xs.at[0], xr.at[slot], (d, b, hc)).wait_recv()

    def got_w(slot):
        remote(wg_ref.at[slot], wg_ref.at[slot], ws.at[0], wr.at[slot], (d, b, hc)).wait_recv()

    for p in zpeers:
        send_x(x_ref, own_x, (d, p, h))
    send_x(x_ref, own_x, (d, b, hy))
    send_x(x_ref, own_x, (d, b, hc))
    for p in dpeers:
        send_w(w_ref, own_w, (p, b, h))
    for p in zpeers:
        send_w(w_ref, own_w, (d, p, h))
    send_w(w_ref, own_w, (d, b, hy))
    send_w(w_ref, own_w, (d, b, hc))
    for f in zfrom:
        slot = xslot(f, h)
        got_x(slot)
        send_x(xg_ref.at[slot], slot, (d, b, hy))
        send_x(xg_ref.at[slot], slot, (d, b, hc))
    for f in zfrom:
        slot = wslot(d, f, h)
        got_w(slot)
        for p in dpeers:
            send_w(wg_ref.at[slot], slot, (p, b, h))
        send_w(wg_ref.at[slot], slot, (d, b, hy))
        send_w(wg_ref.at[slot], slot, (d, b, hc))
    for f in [b] + zfrom:
        slot = xslot(f, hy)
        got_x(slot)
        send_x(xg_ref.at[slot], slot, (d, b, hc))
    for f in [b] + zfrom:
        slot = wslot(d, f, hy)
        got_w(slot)
        for p in dpeers:
            send_w(wg_ref.at[slot], slot, (p, b, h))
        send_w(wg_ref.at[slot], slot, (d, b, hc))
    for g in dfrom:
        for hh in (h, hy):
            for f in [b] + zfrom:
                slot = wslot(g, f, hh)
                got_w(slot)
                send_w(wg_ref.at[slot], slot, (d, b, hc))
    for hh in (hc, hyc):
        for f in [b] + zfrom:
            got_x(xslot(f, hh))
    for g in [d] + dfrom:
        for hh in (hc, hyc):
            for f in [b] + zfrom:
                got_w(wslot(g, f, hh))
    cx.wait()
    cw.wait()
    for c in sent_x + sent_w:
        c.wait_send()


def gather(z, x, w):
    nb, nh, nd = z.n_blk, z.n_head, z.n_dp
    count_x = (nb - 1) + 2 + 2 * (nb - 1) + nb
    count_w = (nd - 1) + (nb - 1) + 2 + (nb - 1) * (nd + 1) + nb * nd + (nd - 1) * 2 * nb
    return pl.pallas_call(
        functools.partial(gather_kernel, z),
        out_shape=(
            jax.ShapeDtypeStruct((z.ns,) + x.shape, x.dtype),
            jax.ShapeDtypeStruct((z.ndev,) + w.shape, w.dtype),
        ),
        in_specs=[pl.BlockSpec(memory_space=pl.ANY)] * 2,
        out_specs=(pl.BlockSpec(memory_space=pl.ANY),) * 2,
        scratch_shapes=[
            pltpu.SemaphoreType.DMA((count_x,)),
            pltpu.SemaphoreType.DMA((z.ns,)),
            pltpu.SemaphoreType.DMA((count_w,)),
            pltpu.SemaphoreType.DMA((z.ndev,)),
            pltpu.SemaphoreType.DMA((2,)),
        ],
        compiler_params=pltpu.CompilerParams(collective_id=0, has_side_effects=True),
        name="gather_inputs",
    )(x, w)


def bias_tile(table, shift):
    i = lax.broadcasted_iota(jnp.int32, (BLOCK, BLOCK), 0)
    j = lax.broadcasted_iota(jnp.int32, (BLOCK, BLOCK), 1)
    dist = j - i + shift
    mag = jnp.abs(dist)
    half = BUCKETS // 2
    out = jnp.broadcast_to(table[0:1, 0:1], (BLOCK, BLOCK))
    for n, limit in enumerate(LIMITS):
        low = table[n + 1 : n + 2, 0:1]
        if shift == 0:
            high = table[half + n + 1 : half + n + 2, 0:1]
            out = jnp.where(mag >= limit, jnp.where(dist > 0, high, low), out)
        else:
            out = jnp.where(mag >= limit, low, out)
    return out


def forward_kernel(
    z, entry_ref, x_ref, w_ref, normed_ref, qkv_ref, p_ref, att_ref,
    slab, wh, gain, far, bias_d, bias_s, k_scr, v_scr, s_scr, sem,
):
    step = pl.program_id(0)
    D = z.D

    @pl.when(step == 0)
    def _():
        d, b, h = place()
        hd = b * z.hb + jnp.minimum(h, z.hb - 1)
        pair = hd // 2
        copies = []
        for m in range(3):
            at = pl.ds(pl.multiple_of(m * D + pair * LANES, LANES), LANES)
            copies.append(pltpu.make_async_copy(w_ref.at[:, :, at], slab.at[m], sem.at[m]))
        copies.append(
            pltpu.make_async_copy(w_ref.at[:, :, pl.ds(4 * D, LANES)], slab.at[3], sem.at[3])
        )
        for c in copies:
            c.start()
        for c in copies:
            c.wait()
        odd = lax.rem(hd, 2) == 1
        for m in range(3):
            rows = flatten_rows(slab[m])
            own = jnp.where(odd, rows[:, HEAD_SIZE:], rows[:, :HEAD_SIZE])
            if m == 0:
                own = own * HEAD_SIZE ** (-0.5)
            wh[:, m * HEAD_SIZE : (m + 1) * HEAD_SIZE] = own.astype(BF16)
        misc = flatten_rows(slab[3])
        gain[...] = jnp.transpose(misc)[z.E : z.E + 1, :]
        wanted = hd * BUCKETS + lax.broadcasted_iota(jnp.int32, (BUCKETS, D), 0)
        pick = (entry_ref[...] == wanted).astype(BF16)
        table = nn(pick, misc.astype(BF16))[:, z.E + 2 : z.E + 3]
        bias_d[...] = bias_tile(table, 0)
        bias_s[...] = bias_tile(table, -BLOCK)
        far[...] = table[BUCKETS // 2 - 1 : BUCKETS // 2, 0:1]

    x = x_ref[...].astype(F32)
    inverse = lax.rsqrt(jnp.mean(x * x, axis=-1, keepdims=True) + EPSILON)
    normed = (x * inverse * gain[...]).astype(BF16)
    normed_ref[...] = normed
    qkv = nn(normed, wh[...]).astype(BF16)
    qkv_ref[...] = qkv
    here = pl.ds(pl.multiple_of(step * BLOCK, BLOCK), BLOCK)
    q = qkv[:, :HEAD_SIZE]
    k_scr[here, :] = qkv[:, HEAD_SIZE : 2 * HEAD_SIZE]
    v_scr[here, :] = qkv[:, 2 * HEAD_SIZE :]

    def at(j):
        return pl.ds(pl.multiple_of(j * BLOCK, BLOCK), BLOCK)

    def score(j, bias, top):
        s = nt(q, k_scr[at(j), :]) + bias
        s_scr[:, at(j)] = s
        return jnp.maximum(top, jnp.max(s, axis=-1, keepdims=True))

    top = jnp.full((BLOCK, 1), -1e30, F32)
    top = lax.fori_loop(0, step - 1, lambda j, t: score(j, far[...], t), top)
    top = lax.fori_loop(
        jnp.maximum(step - 1, 0), step, lambda j, t: score(j, bias_s[...], t), top
    )
    top = score(step, bias_d[...], top)

    def exps(j, total):
        e = jnp.exp(s_scr[:, at(j)] - top)
        s_scr[:, at(j)] = e
        return total + jnp.sum(e, axis=-1, keepdims=True)

    total = lax.fori_loop(0, step + 1, exps, jnp.zeros((BLOCK, 1), F32))
    scale = 1.0 / total

    def values(j, acc):
        p = (s_scr[:, at(j)] * scale).astype(BF16)
        p_ref[0, :, at(j)] = p
        return acc + nn(p, v_scr[at(j), :])

    acc = lax.fori_loop(0, step + 1, values, jnp.zeros((BLOCK, HEAD_SIZE), F32))
    att_ref[...] = acc.astype(BF16)


def attention_forward(z, entries, xg, wg):
    D, S, HS = z.D, z.S, HEAD_SIZE
    row = lambda i: (i, 0)
    return pl.pallas_call(
        functools.partial(forward_kernel, z),
        grid=(z.nq,),
        out_shape=(
            jax.ShapeDtypeStruct((S, D), BF16),
            jax.ShapeDtypeStruct((S, 3 * HS), BF16),
            jax.ShapeDtypeStruct((z.nq, BLOCK, S), BF16),
            jax.ShapeDtypeStruct((S, HS), BF16),
        ),
        in_specs=[
            pl.BlockSpec((1, D), lambda i: (0, 0)),
            pl.BlockSpec((BLOCK, D), row),
            pl.BlockSpec(memory_space=pl.ANY),
        ],
        out_specs=(
            pl.BlockSpec((BLOCK, D), row),
            pl.BlockSpec((BLOCK, 3 * HS), row),
            pl.BlockSpec((1, BLOCK, S), lambda i: (i, 0, 0)),
            pl.BlockSpec((BLOCK, HS), row),
        ),
        scratch_shapes=[
            pltpu.VMEM((4, z.ndev, z.R, LANES), BF16),
            pltpu.VMEM((D, 3 * HS), BF16),
            pltpu.VMEM((1, D), F32),
            pltpu.VMEM((1, 1), F32),
            pltpu.VMEM((BLOCK, BLOCK), F32),
            pltpu.VMEM((BLOCK, BLOCK), F32),
            pltpu.VMEM((S, HS), BF16),
            pltpu.VMEM((S, HS), BF16),
            pltpu.VMEM((BLOCK, S), F32),
            pltpu.SemaphoreType.DMA((4,)),
        ],
        compiler_params=pltpu.CompilerParams(
            dimension_semantics=("arbitrary",), vmem_limit_bytes=48 * 1024 * 1024
        ),
        name="attention_forward",
    )(entries, xg.reshape(S, D), wg)


def middle_kernel(
    z, att_ref, x_ref, w_ref, order_ref, ids_ref, win_ref, wout_ref, cot_ref,
    layer_ref, gmid_ref, gatt_ref, dwo_ref, all_ref,
    win, wout, wo3, misc3, att_in, disp, exp_in, ret, back, route, att_cat, out_acc, gg_acc,
    loc, att_s, att_r, dis_s, dis_r, ret_s, ret_r, all_s, all_r,
):
    d, b, h = place()
    nb, nh, nd, ns = z.n_blk, z.n_head, z.n_dp, z.ns
    D, E, PT, SB, NG = z.D, z.E, z.PT, z.SB, z.NG
    s = b * nh + h
    me = d * ns + s
    g = d * nb + b
    hd = b * z.hb + jnp.minimum(h, z.hb - 1)
    active = h < z.hb
    hy = lax.rem(h + 2, nh)
    hc = h + 1 - 2 * lax.rem(h, 2)
    hyc = lax.rem(hc + 2, nh)

    def seq_peer(k):
        t = lax.rem(s + k, ns)
        return t, (d, t // nh, lax.rem(t, nh))

    def exp_peer(k):
        e = lax.rem(g + k, NG)
        return e, (e // nb, lax.rem(e, nb), h)

    def exp_from(k):
        e = lax.rem(g + NG - k, NG)
        return e, (e // nb, lax.rem(e, nb), h)

    for k in range(1, ns):
        signal(seq_peer(k)[1])
    for k in range(1, nd):
        for kb in range(nb):
            signal((lax.rem(d + k, nd), lax.rem(b + kb, nb), h))

    local = [
        pltpu.make_async_copy(w_ref.at[:, :, pl.ds(3 * D, D)], wo3, loc.at[0]),
        pltpu.make_async_copy(w_ref.at[:, :, pl.ds(4 * D, LANES)], misc3, loc.at[1]),
        pltpu.make_async_copy(win_ref.at[0], win, loc.at[2]),
        pltpu.make_async_copy(wout_ref.at[0], wout, loc.at[3]),
    ]
    for c in local:
        c.start()
    await_barrier(ns - 1 + (nd - 1) * nb)

    def send_att(k):
        t, device = seq_peer(k)
        return remote(att_ref.at[t], att_in.at[hd], att_s.at[k], att_r.at[hd], device)

    @pl.when(active)
    def _():
        for k in range(1, ns):
            send_att(k).start()
        own = pltpu.make_async_copy(att_ref.at[s], att_in.at[hd], loc.at[4])
        own.start()
        own.wait()

    ids_row = ids_ref[pl.ds(me, 1), :]
    order_row = order_ref[...]
    ids_col = jnp.transpose(jnp.broadcast_to(ids_row, (PT, PT)))
    order_col = jnp.transpose(jnp.broadcast_to(order_row, (PT, PT)))
    earlier = (order_col < order_row) & (ids_col == ids_row)
    rank = jnp.sum(earlier.astype(jnp.int32), axis=0, keepdims=True)
    ids2 = jnp.concatenate([ids_row, ids_row], axis=1)
    rank2 = jnp.concatenate([rank, rank], axis=1)
    kk = lax.broadcasted_iota(jnp.int32, (SB, 2 * PT), 0)
    cc = lax.broadcasted_iota(jnp.int32, (SB, 2 * PT), 1)
    low = kk >= z.cap8
    kept = jnp.where(low, kk - z.cap8, kk)
    base = (rank2 == kept) & (kept < z.cap) & (low.astype(jnp.int32) == (cc >= PT).astype(jnp.int32))
    lane = lax.broadcasted_iota(jnp.int32, (1, LANES), 1)
    share = jnp.zeros((1, LANES), F32)
    ids_all = ids_ref[...]
    for e in range(E):
        route[e * SB : (e + 1) * SB, :] = (base & (ids2 == e)).astype(BF16)
        count = jnp.sum((ids_all == e).astype(F32), axis=1, keepdims=True)
        count = jnp.sum(count, axis=0, keepdims=True)
        share = share + jnp.where(lane == e, count, 0.0)
    share = share * (AUX_WEIGHT * E / (ids_all.shape[0] * ids_all.shape[1]))
    chosen = (ids_col[:, :1] == lane)

    local[0].wait()
    local[1].wait()
    wo = flatten_rows(wo3[...]).astype(BF16)
    misc = flatten_rows(misc3[...])
    router = misc.astype(BF16)
    gain = jnp.transpose(misc)[E + 1 : E + 2, :]
    x = x_ref[...].astype(F32)
    cot = cot_ref[...].astype(F32)

    for n in range(HEAD_COUNT):

        @pl.when(jnp.logical_not(active & (hd == n)))
        def _():
            remote(
                att_in.at[n], att_in.at[n], att_s.at[0], att_r.at[n], (d, b, hc)
            ).wait_recv()

        att_cat[:, n * HEAD_SIZE : (n + 1) * HEAD_SIZE] = att_in[n]
    att = att_cat[...]
    middle = x + nn(att, wo)
    inverse = lax.rsqrt(jnp.mean(middle * middle, axis=-1, keepdims=True) + EPSILON)
    routed = (middle * inverse * gain).astype(BF16)
    logits = jnp.where(lane < E, nn(routed, router), -1e30)
    exps = jnp.exp(logits - jnp.max(logits, axis=-1, keepdims=True))
    probs = exps / jnp.sum(exps, axis=-1, keepdims=True)
    gate = jnp.sum(jnp.where(chosen, probs, 0.0), axis=-1, keepdims=True)
    stacked = jnp.concatenate([routed, (gate * cot).astype(BF16)], axis=0)
    disp[...] = nn(route[...], stacked).reshape(E, SB, D).astype(BF16)

    def send_disp(k):
        e, device = exp_peer(k)
        return remote(disp.at[e], exp_in.at[g], dis_s.at[k], dis_r.at[g], device)

    for k in range(1, NG):
        send_disp(k).start()
    exp_in[g] = disp[g]
    local[2].wait()
    local[3].wait()
    for k in range(1, NG):
        e, device = exp_from(k)
        remote(exp_in.at[e], exp_in.at[e], dis_s.at[0], dis_r.at[e], device).wait_recv()
    to_y = remote(exp_in, all_ref.at[h], all_s.at[0], all_r.at[h], (d, b, hy))
    to_c = remote(exp_in, all_ref.at[h], all_s.at[1], all_r.at[h], (d, b, hc))
    to_me = pltpu.make_async_copy(exp_in, all_ref.at[h], loc.at[5])
    to_y.start()
    to_c.start()
    to_me.start()
    slots = exp_in[...].astype(F32)
    rows_in = slots[:, : z.cap8].reshape(NG * z.cap8, D).astype(BF16)
    grad_out = slots[:, z.cap8 :].reshape(NG * z.cap8, D).astype(BF16)
    out_acc[...] = jnp.zeros_like(out_acc)
    gg_acc[...] = jnp.zeros_like(gg_acc)
    chunk = D

    def ff_step(c, carry):
        at = pl.ds(pl.multiple_of(c * chunk, chunk), chunk)
        w1 = win[:, at]
        w2 = wout[at, :]
        pre = nn(rows_in, w1)
        phi, bell = normal_parts(pre)
        hidden = (pre * phi).astype(BF16)
        out_acc[...] += nn(hidden, w2)
        gh = nt(grad_out, w2).astype(BF16).astype(F32)
        gp = (gh * (phi + pre * bell * INV_ROOT_TWO_PI)).astype(BF16)
        gg_acc[...] += nt(gp, w1)
        return carry

    lax.fori_loop(0, z.FF // chunk, ff_step, 0)
    both = jnp.concatenate(
        [out_acc[...].reshape(NG, z.cap8, D), gg_acc[...].reshape(NG, z.cap8, D)], axis=1
    )
    ret[...] = both.astype(BF16)

    def send_ret(k):
        e, device = exp_peer(k)
        return remote(ret.at[e], back.at[g], ret_s.at[k], ret_r.at[g], device)

    for k in range(1, NG):
        send_ret(k).start()
    back[g] = ret[g]
    remote(
        all_ref.at[hy], all_ref.at[hy], all_s.at[0], all_r.at[hy], (d, b, hy)
    ).wait_recv()
    on_c = remote(all_ref.at[hy], all_ref.at[hy], all_s.at[2], all_r.at[hy], (d, b, hc))
    on_c.start()
    for k in range(1, NG):
        e, device = exp_from(k)
        remote(back.at[e], back.at[e], ret_s.at[0], ret_r.at[e], device).wait_recv()
    comb = tn(route[...], back[...].reshape(E * SB, D))
    expert_rows = comb[:PT]
    grad_routed = comb[PT:]
    layer_ref[...] = (middle + gate * expert_rows).astype(BF16)
    grad_gate = jnp.sum(cot * expert_rows, axis=-1, keepdims=True)
    grad_probs = jnp.where(chosen, grad_gate, 0.0) + share
    inner = jnp.sum(probs * grad_probs, axis=-1, keepdims=True)
    grad_logits = (probs * (grad_probs - inner)).astype(BF16)
    grad_routed = grad_routed + nt(grad_logits, router)
    scaled = grad_routed * gain
    mean = jnp.mean(scaled * middle, axis=-1, keepdims=True)
    gmid = cot + inverse * scaled - middle * (inverse * inverse * inverse) * mean
    gmid_ref[...] = gmid
    low_mid = gmid.astype(BF16)
    gatt = nt(low_mid, wo).astype(BF16)
    for n in range(HEAD_COUNT):
        gatt_ref[n] = gatt[:, n * HEAD_SIZE : (n + 1) * HEAD_SIZE]
    term = grad_routed * middle * inverse
    high = term.astype(BF16)
    rest = (term - high.astype(F32)).astype(BF16)
    ones = jnp.broadcast_to((lane == E).astype(BF16), (PT, LANES))
    small = tn(routed, grad_logits) + tn(high, ones) + tn(rest, ones)
    split_rows(dwo_ref, jnp.concatenate([tn(att, low_mid), small], axis=1), z.R)

    to_me.wait()
    for hh in (hc, hyc):
        remote(
            all_ref.at[hh], all_ref.at[hh], all_s.at[0], all_r.at[hh], (d, b, hc)
        ).wait_recv()
    for c in (to_y, to_c, on_c):
        c.wait_send()
    for k in range(1, NG):
        send_disp(k).wait_send()
        send_ret(k).wait_send()

    @pl.when(active)
    def _():
        for k in range(1, ns):
            send_att(k).wait_send()


def middle_part(z, att, x, wg, order, ids, w_in, w_out, cot):
    D, PT, SB, NG, E = z.D, z.PT, z.SB, z.NG, z.E
    dma = pltpu.SemaphoreType.DMA
    vmem = pl.BlockSpec(memory_space=pltpu.VMEM)
    hbm = pl.BlockSpec(memory_space=pl.ANY)
    return pl.pallas_call(
        functools.partial(middle_kernel, z),
        out_shape=(
            jax.ShapeDtypeStruct((PT, D), BF16),
            jax.ShapeDtypeStruct((PT, D), F32),
            jax.ShapeDtypeStruct((HEAD_COUNT, PT, HEAD_SIZE), BF16),
            jax.ShapeDtypeStruct((z.ndev, z.R, D + LANES), BF16),
            jax.ShapeDtypeStruct((z.n_head, NG, SB, D), BF16),
        ),
        in_specs=[hbm, vmem, hbm, vmem, vmem, hbm, hbm, vmem],
        out_specs=(vmem, vmem, vmem, vmem, hbm),
        scratch_shapes=[
            pltpu.VMEM((D, z.FF), BF16),
            pltpu.VMEM((z.FF, D), BF16),
            pltpu.VMEM((z.ndev, z.R, D), BF16),
            pltpu.VMEM((z.ndev, z.R, LANES), BF16),
            pltpu.VMEM((HEAD_COUNT, PT, HEAD_SIZE), BF16),
            pltpu.VMEM((E, SB, D), BF16),
            pltpu.VMEM((NG, SB, D), BF16),
            pltpu.VMEM((NG, SB, D), BF16),
            pltpu.VMEM((E, SB, D), BF16),
            pltpu.VMEM((E * SB, 2 * PT), BF16),
            pltpu.VMEM((PT, D), BF16),
            pltpu.VMEM((NG * z.cap8, D), F32),
            pltpu.VMEM((NG * z.cap8, D), F32),
            dma((6,)),
            dma((z.ns,)),
            dma((HEAD_COUNT,)),
            dma((NG,)),
            dma((NG,)),
            dma((NG,)),
            dma((NG,)),
            dma((3,)),
            dma((z.n_head,)),
        ],
        compiler_params=pltpu.CompilerParams(
            collective_id=1, has_side_effects=True, vmem_limit_bytes=56 * 1024 * 1024
        ),
        name="experts_and_norms",
    )(att.reshape(z.ns, PT, HEAD_SIZE), x, wg, order, ids, w_in, w_out, cot)


def backward_kernel(
    z, gatt_ref, dwo_ref, normed_ref, qkv_ref, p_ref, att_ref, wg_ref, w_ref, x_ref, gmid_ref,
    gtok_ref, gain1_ref, gq_ref, gk_ref, gv_ref, go_ref, table_ref, gain2_ref, router_ref,
    w3, wfull, misc3, normed, qkv, probs, att, do_in, grad_cat, dkv, dqkv, dw, dw3, diag, sub, far,
    dq_in, dw_in, rs_in,
    loc, do_s, do_r, dq_s, dq_r, dw_s, dw_r, rs_s, rs_r,
):
    d, b, h = place()
    nb, nh, nd, ns, nv = z.n_blk, z.n_head, z.n_dp, z.ns, z.ndev
    D, R, PT, HS, E = z.D, z.R, z.PT, HEAD_SIZE, z.E
    s = b * nh + h
    me = d * ns + s
    hd = b * z.hb + jnp.minimum(h, z.hb - 1)
    active = h < z.hb

    def any_peer(k):
        t = lax.rem(me + k, nv)
        return t, (t // ns, lax.rem(t // nh, nb), lax.rem(t, nh))

    def greet(k, carry):
        signal(any_peer(k)[1])
        return carry

    lax.fori_loop(1, nv, greet, 0)
    local = [
        pltpu.make_async_copy(normed_ref, normed, loc.at[0]),
        pltpu.make_async_copy(qkv_ref, qkv, loc.at[1]),
        pltpu.make_async_copy(att_ref, att, loc.at[2]),
        pltpu.make_async_copy(p_ref, probs, loc.at[3]),
        pltpu.make_async_copy(wg_ref.at[:, :, pl.ds(0, 3 * D)], w3, loc.at[4]),
        pltpu.make_async_copy(wg_ref.at[:, :, pl.ds(4 * D, LANES)], misc3, loc.at[5]),
    ]
    for c in local:
        c.start()
    await_barrier(nv - 1)

    def send_do(n):
        hb, hh = n // z.hb, n % z.hb
        return remote(gatt_ref.at[n], do_in.at[s], do_s.at[n], do_r.at[s], (d, hb, hh))

    for n in range(HEAD_COUNT):
        mine = active & (hd == n)

        @pl.when(jnp.logical_not(mine))
        def _():
            send_do(n).start()

        @pl.when(mine)
        def _():
            do_in[s] = gatt_ref[n]

    def send_rs(k):
        t, device = any_peer(k)
        return remote(dwo_ref.at[t], rs_in.at[me], rs_s.at[k], rs_r.at[me], device)

    def start_rs(k, carry):
        send_rs(k).start()
        return carry

    lax.fori_loop(1, nv, start_rs, 0)
    rs_in[me] = dwo_ref[me]
    for c in local:
        c.wait()

    def send_dq(t):
        return remote(
            dqkv.at[t], dq_in.at[hd], dq_s.at[t], dq_r.at[hd], (d, t // nh, lax.rem(t, nh))
        )

    def send_dw(k):
        t, device = any_peer(k)
        slot = d * HEAD_COUNT + hd
        return remote(dw3.at[t], dw_in.at[slot], dw_s.at[k], dw_r.at[slot], device)

    per = BLOCK // PT

    @pl.when(active)
    def _():
        def got_do(k, carry):
            t = lax.rem(s + k, ns)
            remote(
                do_in.at[t], do_in.at[t], do_s.at[0], do_r.at[t], (d, t // nh, lax.rem(t, nh))
            ).wait_recv()
            return carry

        lax.fori_loop(1, ns, got_do, 0)
        dkv[...] = jnp.zeros_like(dkv)
        dw[...] = jnp.zeros_like(dw)
        diag[...] = jnp.zeros_like(diag)
        sub[...] = jnp.zeros_like(sub)
        far[...] = jnp.zeros_like(far)

        def at(j):
            return pl.ds(pl.multiple_of(j * BLOCK, BLOCK), BLOCK)

        def row_block(step, carry):
            i = z.nq - 1 - step
            do = do_in[pl.ds(i * per, per)].reshape(BLOCK, HS)
            delta = jnp.sum(do.astype(F32) * att[at(i), :].astype(F32), axis=-1, keepdims=True)
            q = qkv[at(i), :HS]

            def tile(j, dq):
                k = qkv[at(j), HS : 2 * HS]
                v = qkv[at(j), 2 * HS :]
                p = probs[i, :, at(j)]
                ds = (p.astype(F32) * (nt(do, v) - delta)).astype(BF16)
                dkv[at(j), :HS] += tn(ds, q)
                dkv[at(j), HS:] += tn(p, do)
                return dq + nn(ds, k), ds.astype(F32)

            def far_tile(j, dq):
                dq, ds = tile(j, dq)
                far[...] += jnp.sum(ds, axis=0, keepdims=True)
                return dq

            def sub_tile(j, dq):
                dq, ds = tile(j, dq)
                sub[...] += ds
                return dq

            dq = lax.fori_loop(0, i - 1, far_tile, jnp.zeros((BLOCK, HS), F32))
            dq = lax.fori_loop(jnp.maximum(i - 1, 0), i, sub_tile, dq)
            dq, ds = tile(i, dq)
            diag[...] += ds
            dq = dq * HS ** (-0.5)
            parts = jnp.concatenate([dq, dkv[at(i), :]], axis=1).astype(BF16)
            dw[...] += tn(normed[at(i), :], parts)
            dqkv[pl.ds(i * per, per)] = parts.reshape(per, PT, 3 * HS)
            for u in range(per):
                t = i * per + u

                @pl.when(t != s)
                def _():
                    send_dq(t).start()

                @pl.when(t == s)
                def _():
                    dq_in[hd] = dqkv[t]

            return carry

        lax.fori_loop(0, z.nq, row_block, 0)

        ii = lax.broadcasted_iota(jnp.int32, (BLOCK, BLOCK), 0)
        jj = lax.broadcasted_iota(jnp.int32, (BLOCK, BLOCK), 1)
        lane = lax.broadcasted_iota(jnp.int32, (1, HS), 1)
        sums = jnp.zeros((1, HS), F32)
        half = BUCKETS // 2
        bounds = (0,) + LIMITS + (1 << 30,)
        tile_d, tile_s = diag[...], sub[...]

        def total(values):
            return jnp.sum(jnp.sum(values, axis=0, keepdims=True), axis=1, keepdims=True)

        for n in range(half):
            lo, hi = bounds[n], bounds[n + 1]
            dist = ii - jj
            part = total(
                jnp.where((dist >= lo) & (dist < hi), tile_d, 0.0)
                + jnp.where((dist + BLOCK >= lo) & (dist + BLOCK < hi), tile_s, 0.0)
            )
            if n == half - 1:
                part = part + jnp.sum(far[...], axis=1, keepdims=True)
            sums = sums + jnp.where(lane == n, part, 0.0)
            if n > 0:
                part = total(jnp.where((-dist >= lo) & (-dist < hi), tile_d, 0.0))
                sums = sums + jnp.where(lane == half + n, part, 0.0)
        wide = jnp.concatenate([dw[...], jnp.broadcast_to(sums, (D, HS))], axis=1)
        split_rows(dw3, wide, R)

        def start_dw(k, carry):
            send_dw(k).start()
            return carry

        lax.fori_loop(1, nv, start_dw, 0)
        dw_in[d * HEAD_COUNT + hd] = dw3[me]

    wfull[...] = flatten_rows(w3[...]).astype(BF16)
    gain = jnp.transpose(flatten_rows(misc3[...]))[E : E + 1, :]
    for n in range(HEAD_COUNT):

        @pl.when(jnp.logical_not(active & (hd == n)))
        def _():
            remote(
                dq_in.at[n], dq_in.at[n], dq_s.at[0], dq_r.at[n], (d, n // z.hb, n % z.hb)
            ).wait_recv()

        part = dq_in[n]
        for m in range(3):
            grad_cat[:, m * D + n * HS : m * D + (n + 1) * HS] = part[:, m * HS : (m + 1) * HS]
    grad_normed = nt(grad_cat[...], wfull[...])
    x = x_ref[...].astype(F32)
    inverse = lax.rsqrt(jnp.mean(x * x, axis=-1, keepdims=True) + EPSILON)
    scaled = grad_normed * gain
    mean = jnp.mean(scaled * x, axis=-1, keepdims=True)
    grad_in = inverse * scaled - x * (inverse * inverse * inverse) * mean
    gtok_ref[...] = (gmid_ref[...] + grad_in).astype(BF16)

    def got_rs(k, carry):
        t, device = any_peer(k)
        remote(rs_in.at[t], rs_in.at[t], rs_s.at[0], rs_r.at[t], device).wait_recv()
        return carry

    lax.fori_loop(1, nv, got_rs, 0)
    acc = lax.fori_loop(
        0, nv, lambda t, a: a + rs_in[t].astype(F32), jnp.zeros((R, D + LANES), F32)
    )
    go_ref[...] = acc[:, :D]
    router_ref[...] = acc[:, D : D + E]
    gain2_ref[...] = acc[:, D + E : D + E + 1]

    for dd in range(nd):
        for n in range(HEAD_COUNT):

            @pl.when(jnp.logical_not(active & (hd == n) & (d == dd)))
            def _():
                slot = dd * HEAD_COUNT + n
                remote(
                    dw_in.at[slot], dw_in.at[slot], dw_s.at[0], dw_r.at[slot],
                    (dd, n // z.hb, n % z.hb),
                ).wait_recv()

    lane = lax.broadcasted_iota(jnp.int32, (1, BUCKETS), 1)
    slot_lane = lax.broadcasted_iota(jnp.int32, (1, z.RL), 1)
    own_table = jnp.zeros((1, z.RL), F32)
    first = jnp.zeros((R, 1), F32)
    w_own = w_ref[...].astype(F32)
    for n in range(HEAD_COUNT):
        part = dw_in[n].astype(F32)
        for dd in range(1, nd):
            part = part + dw_in[dd * HEAD_COUNT + n].astype(F32)
        for m, out in enumerate((gq_ref, gk_ref, gv_ref)):
            cols = part[:, m * HS : (m + 1) * HS]
            out[:, n * HS : (n + 1) * HS] = cols
            first = first + jnp.sum(
                cols * w_own[:, m * D + n * HS : m * D + (n + 1) * HS], axis=-1, keepdims=True
            )
        line = part[0:1, 3 * HS : 3 * HS + BUCKETS]
        for k in range(z.RL):
            hit = lane + n * BUCKETS == me * z.RL + k
            value = jnp.sum(jnp.where(hit, line, 0.0), axis=1, keepdims=True)
            own_table = own_table + jnp.where(slot_lane == k, value, 0.0)
    gain1_ref[...] = first / w_own[:, 4 * D + E : 4 * D + E + 1]
    table_ref[...] = own_table

    def sent_rs(k, carry):
        send_rs(k).wait_send()
        return carry

    lax.fori_loop(1, nv, sent_rs, 0)
    for n in range(HEAD_COUNT):

        @pl.when(jnp.logical_not(active & (hd == n)))
        def _():
            send_do(n).wait_send()

    @pl.when(active)
    def _():
        def sent_dq(k, carry):
            send_dq(lax.rem(s + k, ns)).wait_send()
            return carry

        lax.fori_loop(1, ns, sent_dq, 0)

        def sent_dw(k, carry):
            send_dw(k).wait_send()
            return carry

        lax.fori_loop(1, nv, sent_dw, 0)


def attention_backward(z, gatt, dwo, normed, qkv, probs, att, wg, w_own, x, gmid):
    D, R, PT, S, HS, E = z.D, z.R, z.PT, z.S, HEAD_SIZE, z.E
    dma = pltpu.SemaphoreType.DMA
    vmem = pl.BlockSpec(memory_space=pltpu.VMEM)
    hbm = pl.BlockSpec(memory_space=pl.ANY)
    return pl.pallas_call(
        functools.partial(backward_kernel, z),
        out_shape=(
            jax.ShapeDtypeStruct((PT, D), BF16),
            jax.ShapeDtypeStruct((R, 1), F32),
            jax.ShapeDtypeStruct((R, D), F32),
            jax.ShapeDtypeStruct((R, D), F32),
            jax.ShapeDtypeStruct((R, D), F32),
            jax.ShapeDtypeStruct((R, D), F32),
            jax.ShapeDtypeStruct((1, z.RL), F32),
            jax.ShapeDtypeStruct((R, 1), F32),
            jax.ShapeDtypeStruct((R, E), F32),
        ),
        in_specs=[vmem, vmem, hbm, hbm, hbm, hbm, hbm, vmem, vmem, vmem],
        out_specs=(vmem,) * 9,
        scratch_shapes=[
            pltpu.VMEM((z.ndev, R, 3 * D), BF16),
            pltpu.VMEM((D, 3 * D), BF16),
            pltpu.VMEM((z.ndev, R, LANES), BF16),
            pltpu.VMEM((S, D), BF16),
            pltpu.VMEM((S, 3 * HS), BF16),
            pltpu.VMEM((z.nq, BLOCK, S), BF16),
            pltpu.VMEM((S, HS), BF16),
            pltpu.VMEM((z.ns, PT, HS), BF16),
            pltpu.VMEM((PT, 3 * D), BF16),
            pltpu.VMEM((S, 2 * HS), F32),
            pltpu.VMEM((z.ns, PT, 3 * HS), BF16),
            pltpu.VMEM((D, 3 * HS), F32),
            pltpu.VMEM((z.ndev, R, 4 * HS), BF16),
            pltpu.VMEM((BLOCK, BLOCK), F32),
            pltpu.VMEM((BLOCK, BLOCK), F32),
            pltpu.VMEM((1, BLOCK), F32),
            pltpu.VMEM((HEAD_COUNT, PT, 3 * HS), BF16),
            pltpu.VMEM((z.n_dp * HEAD_COUNT, R, 4 * HS), BF16),
            pltpu.VMEM((z.ndev, R, D + LANES), BF16),
            dma((6,)),
            dma((HEAD_COUNT,)),
            dma((z.ns,)),
            dma((z.ns,)),
            dma((HEAD_COUNT,)),
            dma((z.ndev,)),
            dma((z.n_dp * HEAD_COUNT,)),
            dma((z.ndev,)),
            dma((z.ndev,)),
        ],
        compiler_params=pltpu.CompilerParams(
            collective_id=2, has_side_effects=True, vmem_limit_bytes=58 * 1024 * 1024
        ),
        name="attention_backward",
    )(
        gatt, dwo, normed, qkv, probs, att, wg, w_own, x, gmid
    )


def expert_kernel(z, slots_ref, win_ref, wout_ref, gin_ref, gout_ref, rows_in, rows_t, grad_out):
    @pl.when(pl.program_id(0) == 0)
    def _():
        for n in range(z.n_head):
            slots = slots_ref[n].astype(F32)
            at = slice(n * z.NG * z.cap8, (n + 1) * z.NG * z.cap8)
            rows = slots[:, : z.cap8].reshape(z.NG * z.cap8, z.D)
            rows_in[at, :] = rows.astype(BF16)
            grad_out[at, :] = slots[:, z.cap8 :].reshape(z.NG * z.cap8, z.D).astype(BF16)
        rows_t[...] = jnp.transpose(rows_in[...])

    w1 = win_ref[0]
    w2 = wout_ref[0]
    pre = nn(rows_in[...], w1)
    phi, bell = normal_parts(pre)
    hidden = (pre * phi).astype(BF16)
    gh = nt(grad_out[...], w2).astype(BF16).astype(F32)
    gp = (gh * (phi + pre * bell * INV_ROOT_TWO_PI)).astype(BF16)
    gin_ref[0] = nn(rows_t[...], gp)
    gout_ref[0] = tn(hidden, grad_out[...])


def expert_weights(z, slots, w_in, w_out):
    chunk = 512
    total = z.n_head * z.NG * z.cap8
    in_chunk = pl.BlockSpec((1, z.D, chunk), lambda i: (0, 0, i))
    out_chunk = pl.BlockSpec((1, chunk, z.D), lambda i: (0, i, 0))
    return pl.pallas_call(
        functools.partial(expert_kernel, z),
        grid=(z.FF // chunk,),
        out_shape=(
            jax.ShapeDtypeStruct((1, z.D, z.FF), F32),
            jax.ShapeDtypeStruct((1, z.FF, z.D), F32),
        ),
        in_specs=[pl.BlockSpec(memory_space=pltpu.VMEM), in_chunk, out_chunk],
        out_specs=(in_chunk, out_chunk),
        scratch_shapes=[
            pltpu.VMEM((total, z.D), BF16),
            pltpu.VMEM((z.D, total), BF16),
            pltpu.VMEM((total, z.D), BF16),
        ],
        compiler_params=pltpu.CompilerParams(
            dimension_semantics=("arbitrary",), vmem_limit_bytes=48 * 1024 * 1024
        ),
        name="expert_weight_grads",
    )(slots, w_in, w_out)


def local(
    sizes,
    tokens,
    order,
    expert_ids,
    norm1_gain,
    w_query,
    w_key,
    w_value,
    w_attn_out,
    rel_table,
    norm2_gain,
    w_router,
    w_in,
    w_out,
    cotangent,
):
    R, D = w_query.shape
    E = w_router.shape[1]
    z = Sizes(*sizes, R, D, E, w_in.shape[2], tokens.shape[1])
    rel = jnp.pad(rel_table, (0, R - rel_table.shape[0]))
    misc = jnp.concatenate(
        [w_router, norm1_gain[:, None], norm2_gain[:, None], rel[:, None]], axis=1
    )
    misc = jnp.pad(misc, ((0, 0), (0, LANES - misc.shape[1])))
    w_own = jnp.concatenate([w_query, w_key, w_value, w_attn_out, misc], axis=1)
    row = np.arange(D)
    entries = np.where(row % R < z.RL, row // R * z.RL + row % R, -1).astype(np.int32)[None, :]
    ids = expert_ids.reshape(-1, z.PT)
    x = tokens.reshape(z.PT, D)
    cot = cotangent.reshape(z.PT, D)

    xg, wg = gather(z, x, w_own)
    normed, qkv, probs, att = attention_forward(z, jnp.asarray(entries), xg, wg)
    layer, gmid, gatt, dwo, slots = middle_part(z, att, x, wg, order, ids, w_in, w_out, cot)
    gtok, gain1, gq, gk, gv, go, table, gain2, router = attention_backward(
        z, gatt, dwo, normed, qkv, probs, att, wg, w_own, x, gmid
    )
    g_in, g_out = expert_weights(z, slots, w_in, w_out)
    return (
        layer.reshape(tokens.shape),
        gtok.reshape(tokens.shape),
        gain1.reshape(R),
        gq,
        gk,
        gv,
        go,
        table.reshape(z.RL),
        gain2.reshape(R),
        router,
        g_in,
        g_out,
    )


def solution(mesh):
    everywhere = ("dp", "blk", "head")
    rows, table = P(everywhere), P(everywhere, None)
    tokens = P("dp", ("blk", "head"), None)
    expert = P(("dp", "blk"), None, None)
    in_specs = (
        tokens,
        P("dp", ("blk", "head")),
        P(),
        rows,
        table,
        table,
        table,
        table,
        rows,
        rows,
        table,
        expert,
        expert,
        tokens,
    )
    out_specs = (
        tokens, tokens, rows, table, table, table, table, rows, rows, table, expert, expert
    )
    sizes = (mesh.shape["dp"], mesh.shape["blk"], mesh.shape["head"])
    return jax.shard_map(
        functools.partial(local, sizes),
        mesh=mesh,
        in_specs=in_specs,
        out_specs=out_specs,
        check_vma=False,
    )
```

time: 1870 us -> 270 us (0.14)
  waiting for transfers between devices: 1250 us -> 0 us
  Pallas kernels: 0 us -> 249 us
  blocking collectives: 207 us -> 0 us
  local copies, waits for them, and re-layouts: 194 us -> 16.8 us
  matrix products: 82.2 us -> 0 us
  loops' own time: 48.8 us -> 0 us
  other arithmetic: 40.3 us -> 2.75 us
  starting transfers between devices: 23 us -> 0 us
    reduce_scatter x7 -> x0, waiting for transfers between devices: 1010 us -> none  [the longest x1 332 us: local(): lax.psum_scatter(grad_keys.reshape(seq_count, key_block_count * block_row...]
    pallas_call x0 -> x5, Pallas kernels: none -> 249 us  [the longest x1 81.5 us: attention_backward(): pl.pallas_call(functools.partial(backward_kernel, z), out_shape=(jax.Shap...]
    psum x1 -> x0, waiting for transfers between devices: 110 us -> none  [local(): lax.psum(grad_w_in.astype(jnp.bfloat16), 'head').astype(jnp.float32)]
    all_gather x4 -> x0, waiting for transfers between devices: 106 us -> none  [the longest x1 48 us: local(): lax.all_gather(w_value, ('dp', 'blk', 'head'), axis=0, tiled=True)]
    all_gather x4 -> x0, blocking collectives: 86.4 us -> none  [the longest x1 41.1 us: local(): lax.all_gather(w_router, ('dp', 'blk', 'head'), axis=0, tiled=True)]
    dot_general x39 -> x0, matrix products: 82.2 us -> none  [the longest x1 8.49 us: local(): jnp.einsum('necd,edf->necf', grouped, w_in, preferred_element_type=jnp.fl...]
    unnamed x2 -> x0, blocking collectives: 80.6 us -> none
    reshape x14 -> x0, local copies, waits for them, and re-layouts: 61.5 us -> none  [the longest x5 58.5 us: bias_square(): repeated[:, :block_rows * (2 * block_rows - 1)]]
  transfers between devices with their start and end apart: 18 -> 0, of which waited for: 13 -> 0; matrix products, arithmetic and copies ran while one was open for 8% -> 0% of each run, Pallas kernels for 0% -> 0%
where the time goes in v1:
time: 270 us
  Pallas kernels  249 us (92%)
  local copies, waits for them, and re-layouts  16.8 us (6%)
  other arithmetic  2.75 us (1%)
    pallas_call x1, Pallas kernels, attention_backward(): pl.pallas_call(functools.partial(backward_kernel, z), out_shape=(jax.Shap...  81.5 us
    pallas_call x1, Pallas kernels, middle_part(): pl.pallas_call(functools.partial(middle_kernel, z), out_shape=(jax.ShapeD...  58.5 us
    pallas_call x1, Pallas kernels, gather(): pl.pallas_call(functools.partial(gather_kernel, z), out_shape=(jax.ShapeD...  56.9 us
    pallas_call x1, Pallas kernels, attention_forward(): pl.pallas_call(functools.partial(forward_kernel, z), grid=(z.nq,), out_sh...  29.2 us
    pallas_call x1, Pallas kernels, expert_weights(): pl.pallas_call(functools.partial(expert_kernel, z), grid=(z.FF // chunk,)...  23.2 us
    unnamed x39, local copies, waits for them, and re-layouts  14.5 us

profile of v1, /device:TPU:0, one launch (start us, length us, event | category | flops | bytes accessed | tf_op | source)
XLA Modules:
  0.0 269.5 jit_solution(5144001306469601839)
XLA Ops:
  0.6 0.7 pad_bitcast_fusion
  1.3 0.1 copy.35
  1.4 0.7 copy.33
  2.2 0.7 copy.34
  2.9 0.8 copy.32
  3.7 0.8 constant_dynamic-update-slice_fusion.4
  4.4 0.8 constant_dynamic-update-slice_fusion.3
  5.2 0.8 constant_dynamic-update-slice_fusion.2
  6.0 0.8 constant_dynamic-update-slice_fusion.1
  6.7 0.1 constant_dynamic-update-slice_fusion.w_ref
  6.8 0.0 copy-start.5
  6.8 0.7 copy-done.5
  7.5 56.9 %gather_inputs.1 = (bf16[16,128,768]{2,1,0:T(8,128)(2,1)}, bf16[32,24,3200]{2,1,0:T(8,128)(2,1)}) custom-call(bf16[128,768]{1,0:T(8,128)(2,1)} %bitcast.14, bf16[24,3200]{1,0:T(8,128)(2,1)} %copy-done.5), custom_call_target="tpu_custom_call" | custom-call | tf_op jit(solution)/shard_map/gather_inputs/pallas_call | solution.py:209
  64.4 0.0 copy-start.4
  64.4 0.7 copy-done.4
  65.1 29.2 %attention_forward.1 = (bf16[2048,768]{1,0:T(8,128)(2,1)S(1)}, bf16[2048,192]{1,0:T(8,128)(2,1)S(1)}, bf16[8,256,2048]{2,1,0:T(8,128)(2,1)}, bf16[2048,64]{1,0:T(8,128)(2,1)S(1)}) custom-call(s32[1,768]{1,0:T(1,128)S(1)} %copy-done.4, bf16[2048,768]{1,0:T(8,128)(2,1)} %bitcast.13, bf16[32,24,3200]{2,1,0:T(8,128)(2,1)} %get-tuple-element.35.w_ref.wg_ref), custom_call_target="tpu_custom_call" | custom-call | tf_op jit(solution)/shard_map/attention_forward/pallas_call | solution.py:331
  94.3 0.0 copy-start
  94.3 1.7 copy-done
  95.9 0.0 copy-start.2
  95.9 0.8 copy-done.2
  96.7 0.0 copy-start.3
  96.7 1.1 copy-done.3
  97.8 58.5 %experts_and_norms.1 = (bf16[128,768]{1,0:T(8,128)(2,1)}, f32[128,768]{1,0:T(8,128)}, bf16[12,128,64]{2,1,0:T(8,128)(2,1)}, bf16[32,24,896]{2,1,0:T(8,128)(2,1)}, bf16[4,8,48,768]{3,2,1,0:T(8,128)(2,1)}) custom-call(bf16[16,128,64]{2,1,0:T(8,128)(2,1)} %bitcast.12, bf16[128,768]{1,0:T(8,128)(2,1)} %bitcast.15, ...), custom_call_target="tpu_custom_call" | custom-call | tf_op jit(solution)/shard_map/experts_and_norms/pallas_call | solution.py:586
  156.3 0.0 copy-start.1
  156.3 81.5 %attention_backward.1 = (bf16[128,768]{1,0:T(8,128)(2,1)}, f32[24,1]{1,0:T(8,128)}, f32[24,768]{1,0:T(8,128)}, f32[24,768]{1,0:T(8,128)}, f32[24,768]{1,0:T(8,12...) custom-call(bf16[12,128,64]{2,1,0:T(8,128)(2,1)} %get-tuple-element.38.gatt_ref, ...), custom_call_target="tpu_custom_call" | custom-call | tf_op jit(solution)/shard_map/attention_backward/pallas_call | solution.py:904
  237.8 1.3 reduce
  239.2 1.3 reduce.1
  240.5 1.4 copy.36
  241.9 0.0 copy-done.1
  241.9 0.0 copy-start.6
  241.9 0.0 copy-start.7
  241.9 0.0 copy-start.11
  241.9 0.0 copy-start.10
  241.9 0.0 copy-start.9
  241.9 0.0 copy-start.8
  241.9 0.0 copy-start.12
  241.9 23.2 %expert_weight_grads.1 = (f32[1,768,3072]{2,1,0:T(8,128)}, f32[1,3072,768]{2,1,0:T(8,128)}) custom-call(bf16[4,8,48,768]{3,2,1,0:T(8,128)(2,1)S(1)} %copy-done.1, bf16[1,768,3072]{2,1,0:T(8,128)(2,1)} %win_ref.3, bf16[1,3072,768]{2,1,0:T(8,128)(2,1)} %wout_ref.3), custom_call_target="tpu_custom_call" | custom-call | tf_op jit(solution)/shard_map/expert_weight_grads/pallas_call | solution.py:985
  265.1 0.0 copy-done.6
  265.1 0.7 copy.48
  265.8 0.0 copy-done.7
  265.8 0.7 copy.49
  266.5 0.0 copy-done.11
  266.5 0.6 copy.50
  267.1 0.0 copy-done.10
  267.1 0.6 copy.51
  267.8 0.0 copy-done.9
  267.8 0.6 copy.52
  268.4 0.0 copy-done.8
  268.4 0.6 copy.53
  269.0 0.0 copy-done.12
  269.0 0.5 copy.54
Async XLA Ops:
  6.8 0.7 copy-start.5
  64.4 0.7 copy-start.4
  94.3 1.7 copy-start
  95.9 0.8 copy-start.2
  96.7 1.1 copy-start.3
  156.3 85.6 %copy-start.1 = (bf16[4,8,48,768]{3,2,1,0:T(8,128)(2,1)S(1)}, bf16[4,8,48,768]{3,2,1,0:T(8,128)(2,1)}, u32[]{:S(2)}) copy-start(bf16[4,8,48,768]{3,2,1,0:T(8,128)(2,1)} %get-tuple-element.53.slots_ref) | copy-start | bytes 7077892
  241.9 23.3 %copy-start.6 = (bf16[128,768]{1,0:T(8,128)(2,1)S(1)}, bf16[128,768]{1,0:T(8,128)(2,1)}, u32[]{:S(2)}) copy-start(bf16[128,768]{1,0:T(8,128)(2,1)} %get-tuple-element.37) | copy-start | bytes 589828
  241.9 23.9 %copy-start.7 = (bf16[128,768]{1,0:T(8,128)(2,1)S(1)}, bf16[128,768]{1,0:T(8,128)(2,1)}, u32[]{:S(2)}) copy-start(bf16[128,768]{1,0:T(8,128)(2,1)} %get-tuple-element.44) | copy-start | bytes 589828
  241.9 24.6 %copy-start.11 = (f32[24,768]{1,0:T(8,128)S(1)}, f32[24,768]{1,0:T(8,128)}, u32[]{:S(2)}) copy-start(f32[24,768]{1,0:T(8,128)} %get-tuple-element.95) | copy-start | bytes 221188
  241.9 25.2 %copy-start.10 = (f32[24,768]{1,0:T(8,128)S(1)}, f32[24,768]{1,0:T(8,128)}, u32[]{:S(2)}) copy-start(f32[24,768]{1,0:T(8,128)} %get-tuple-element.96) | copy-start | bytes 221188
  241.9 25.9 %copy-start.9 = (f32[24,768]{1,0:T(8,128)S(1)}, f32[24,768]{1,0:T(8,128)}, u32[]{:S(2)}) copy-start(f32[24,768]{1,0:T(8,128)} %get-tuple-element.97) | copy-start | bytes 221188
  241.9 26.5 %copy-start.8 = (f32[24,768]{1,0:T(8,128)S(1)}, f32[24,768]{1,0:T(8,128)}, u32[]{:S(2)}) copy-start(f32[24,768]{1,0:T(8,128)} %get-tuple-element.98) | copy-start | bytes 221188
  241.9 27.1 %copy-start.12 = (f32[1,12]{1,0:T(1,128)S(1)}, f32[1,12]{1,0:T(1,128)}, u32[]{:S(2)}) copy-start(f32[1,12]{1,0:T(1,128)} %get-tuple-element.50) | copy-start | bytes 148

commit v2 on v1

v2 whole, which is shorter than its diff:
```python
import functools
import itertools

import jax
import jax.numpy as jnp
import numpy as np
from jax import lax
from jax.experimental import pallas as pl
from jax.experimental.pallas import tpu as pltpu
from jax.sharding import PartitionSpec as P

HEAD_COUNT = 12
HEAD_SIZE = 64
BUCKETS = 32
BLOCK = 256
EPSILON = 1e-06
AUX_WEIGHT = 1.0
LIMITS = (1, 2, 3, 4, 5, 6, 7, 8, 12, 16, 23, 32, 46, 64, 91)
INV_ROOT_TWO = 0.7071067811865476
INV_ROOT_TWO_PI = 0.3989422804014327
LANES = 128
MESH = pl.DeviceIdType.MESH
F32 = jnp.float32
BF16 = jnp.bfloat16


class Sizes:
    def __init__(self, n_dp, n_blk, n_head, rows, width, experts, hidden, piece):
        self.n_dp, self.n_blk, self.n_head = n_dp, n_blk, n_head
        self.ndev = n_dp * n_blk * n_head
        self.ns = n_blk * n_head
        self.R, self.D, self.E, self.FF, self.PT = rows, width, experts, hidden, piece
        self.S = piece * self.ns
        self.nq = self.S // BLOCK
        self.hb = HEAD_COUNT // n_blk
        self.cap = (5 * piece + 4 * experts - 1) // (4 * experts)
        self.cap8 = (self.cap + 7) // 8 * 8
        self.NG = n_dp * n_blk
        self.RL = HEAD_COUNT * BUCKETS // self.ndev
        assert self.hb <= n_head and self.hb * n_blk == HEAD_COUNT
        assert experts == self.NG and n_head == 4


def nt(a, b):
    return lax.dot_general(a, b, (((1,), (1,)), ((), ())), preferred_element_type=F32)


def tn(a, b):
    return lax.dot_general(a, b, (((0,), (0,)), ((), ())), preferred_element_type=F32)


def nn(a, b):
    return jnp.dot(a, b, preferred_element_type=F32)


def place():
    return lax.axis_index("dp"), lax.axis_index("blk"), lax.axis_index("head")


def signal(device):
    pl.semaphore_signal(
        pltpu.get_barrier_semaphore(), inc=1, device_id=device, device_id_type=MESH
    )


def await_barrier(count):
    pl.semaphore_wait(pltpu.get_barrier_semaphore(), count)


def remote(src, dst, send, recv, device):
    return pltpu.make_async_remote_copy(
        src_ref=src, dst_ref=dst, send_sem=send, recv_sem=recv, device_id=device, device_id_type=MESH
    )


def flatten_rows(blocks):
    count, rows, lanes = blocks.shape
    wide = blocks.astype(F32)
    if rows % 8 == 0:
        return wide.reshape(count * rows, lanes)
    return jnp.concatenate([wide[i] for i in range(count)], axis=0)


def split_rows(dst_ref, values, rows):
    count = values.shape[0] // rows
    if rows % 8 == 0:
        dst_ref[...] = values.reshape(count, rows, values.shape[1]).astype(dst_ref.dtype)
    else:
        for i in range(count):
            dst_ref[i] = values[i * rows : (i + 1) * rows].astype(dst_ref.dtype)


def normal_parts(v):
    bell = jnp.exp(-0.5 * v * v)
    t = 1.0 / (1.0 + (0.3275911 * INV_ROOT_TWO) * jnp.abs(v))
    poly = t * (
        0.254829592
        + t * (-0.284496736 + t * (1.421413741 + t * (-1.453152027 + t * 1.061405429)))
    )
    tail = 0.5 * poly * bell
    return jnp.where(v >= 0, 1.0 - tail, tail), bell


def bias_tile(table, shift):
    j = lax.broadcasted_iota(jnp.int32, (BLOCK, BLOCK), 0)
    i = lax.broadcasted_iota(jnp.int32, (BLOCK, BLOCK), 1)
    dist = j - i + shift
    mag = jnp.abs(dist)
    half = BUCKETS // 2
    out = jnp.broadcast_to(table[0:1, 0:1], (BLOCK, BLOCK))
    for n, limit in enumerate(LIMITS):
        low = table[n + 1 : n + 2, 0:1]
        if shift == 0:
            high = table[half + n + 1 : half + n + 2, 0:1]
            out = jnp.where(mag >= limit, jnp.where(dist > 0, high, low), out)
        else:
            out = jnp.where(mag >= limit, low, out)
    return out


class Spread:
    def __init__(self, z, src, dst, send, recv, y_first, lanes):
        self.z, self.src, self.dst, self.send, self.recv = z, src, dst, send, recv
        self.lanes = lanes
        d, b, h = place()
        self.at = (d, b, h)
        nb, nh, nd = z.n_blk, z.n_head, z.n_dp
        self.hy = lax.rem(h + 2, nh)
        self.hc = h + 1 - 2 * lax.rem(h, 2)
        self.hyc = lax.rem(self.hc + 2, nh)
        self.zto = [lax.rem(b + k, nb) for k in range(1, nb)]
        self.zfrom = [lax.rem(b + nb - k, nb) for k in range(1, nb)]
        dto = [lax.rem(d + k, nd) for k in range(1, nd)]
        dfrom = [lax.rem(d + nd - k, nd) for k in range(1, nd)]
        ys = ([(d, self.hy)], [(d, self.hy)])
        xs = ([(p, h) for p in dto], [(p, h) for p in dfrom])
        self.first, self.second = (ys, xs) if y_first else (xs, ys)
        if y_first:
            self.second_slots = [(p, hh) for p in dfrom for hh in (h, self.hy)]
        else:
            self.second_slots = [(p, self.hy) for p in [d] + dfrom]
        self.core_slots = [(p, hh) for p in [d] + dfrom for hh in (self.hc, self.hyc)]
        self.copies = []

    def slot(self, dd, bb, hh):
        return (dd * self.z.n_blk + bb) * self.z.n_head + hh

    def put(self, own, slot, device):
        src = self.src if own else self.dst.at[slot, :, self.lanes]
        c = remote(
            src, self.dst.at[slot, :, self.lanes], self.send.at[len(self.copies)],
            self.recv.at[slot], device,
        )
        self.copies.append(c)
        c.start()

    def got(self, slot):
        ref = self.dst.at[slot, :, self.lanes]
        d, b, h = self.at
        remote(ref, ref, self.send.at[0], self.recv.at[slot], (d, b, self.hc)).wait_recv()

    def steps(self):
        d, b, h = self.at

        def begin():
            mine = self.slot(d, b, h)
            for p in self.zto:
                self.put(True, mine, (d, p, h))
            for dd, hh in self.first[0] + self.second[0] + [(d, self.hc)]:
                self.put(True, mine, (dd, b, hh))

        def blk_arrival(f):
            slot = self.slot(d, f, h)
            self.got(slot)
            for dd, hh in self.first[0] + self.second[0] + [(d, self.hc)]:
                self.put(False, slot, (dd, b, hh))

        def first_arrival(p, f):
            slot = self.slot(p[0], f, p[1])
            self.got(slot)
            for dd, hh in self.second[0] + [(d, self.hc)]:
                self.put(False, slot, (dd, b, hh))

        def second_arrival(p, f):
            slot = self.slot(p[0], f, p[1])
            self.got(slot)
            self.put(False, slot, (d, b, self.hc))

        out = [begin]
        for f in self.zfrom:
            out.append(functools.partial(blk_arrival, f))
        for p in self.first[1]:
            for f in [b] + self.zfrom:
                out.append(functools.partial(first_arrival, p, f))
        for p in self.second_slots:
            for f in [b] + self.zfrom:
                out.append(functools.partial(second_arrival, p, f))
        return out

    def finish(self):
        d, b, h = self.at
        for p in self.core_slots:
            for f in [b] + self.zfrom:
                self.got(self.slot(p[0], f, p[1]))
        for c in self.copies:
            c.wait_send()


def spread_copies(z, y_first):
    nb, nd = z.n_blk, z.n_dp
    peers = 1 + nd - 1 + 1
    first = 1 if y_first else nd - 1
    second = peers - 1 - first
    second_slots = 2 * (nd - 1) if y_first else nd
    return nb - 1 + peers + (nb - 1) * peers + first * nb * (second + 1) + second_slots * nb


def forward_kernel(
    z, entry_ref, x_ref, wq_ref, wk_ref, wv_ref, wo_ref, router_ref, rows_ref, rel_ref,
    wg_ref, normed_ref, qkv_ref, p_ref, attl_ref, att_out,
    w_own, slices, slices_in, xg, wh, bias_d, bias_s, normed, qkv, v_t, s_scr, p_scr, attl, att_scr,
    xs, xr, ss, sr, was, war, wbs, wbr, ats, atr, loc,
):
    d, b, h = place()
    nb, nh, nd, ns, nv = z.n_blk, z.n_head, z.n_dp, z.ns, z.ndev
    D, R, E, PT, HS = z.D, z.R, z.E, z.PT, HEAD_SIZE
    s = b * nh + h
    me = d * ns + s
    hd = b * z.hb + jnp.minimum(h, z.hb - 1)
    active = h < z.hb
    hy = lax.rem(h + 2, nh)
    hc = h + 1 - 2 * lax.rem(h, 2)
    hyc = lax.rem(hc + 2, nh)

    def any_peer(k):
        t = lax.rem(me + k, nv)
        return t, (t // ns, lax.rem(t // nh, nb), lax.rem(t, nh))

    def greet(k, carry):
        signal(any_peer(k)[1])
        return carry

    lax.fori_loop(1, nv, greet, 0)

    eye = lax.broadcasted_iota(jnp.int32, (R, R), 0) == lax.broadcasted_iota(jnp.int32, (R, R), 1)
    row_of = lax.broadcasted_iota(jnp.int32, (LANES, R), 0)
    gains = jnp.where(
        row_of == E, rows_ref[0:1, :], jnp.where(row_of == E + 1, rows_ref[1:2, :], 0.0)
    )
    gains = jnp.where(row_of == E + 2, rel_ref[...], gains)
    misc = nt(eye.astype(BF16), gains.astype(BF16))
    lane = lax.broadcasted_iota(jnp.int32, (R, LANES), 1)
    w_own[:, 4 * D :] = misc.astype(BF16)
    w_own[:, 4 * D : 4 * D + E] = router_ref[...]
    for m, ref in enumerate((wq_ref, wk_ref, wv_ref, wo_ref)):
        w_own[:, m * D : (m + 1) * D] = ref[...]
    for n in range(HEAD_COUNT):
        at = slice(n * HS, (n + 1) * HS)
        slices[n] = jnp.concatenate(
            [wq_ref[:, at], wk_ref[:, at], wv_ref[:, at], misc[:, E : E + HS].astype(BF16)], axis=1
        )
    save_w = pltpu.make_async_copy(w_own, wg_ref.at[me], loc.at[0])
    save_w.start()
    await_barrier(nv - 1)

    def send_slice(dd, n):
        k = dd * HEAD_COUNT + n
        return remote(
            slices.at[n], slices_in.at[me], ss.at[k], sr.at[me], (dd, n // z.hb, n % z.hb)
        )

    def is_me(dd, n):
        return active & (hd == n) & (d == dd)

    def for_slices(action):
        for dd in range(nd):
            for n in range(HEAD_COUNT):
                pl.when(jnp.logical_not(is_me(dd, n)))(functools.partial(action, dd, n))

    copies = []

    def xslot(bb, hh):
        return bb * nh + hh

    def put(src, slot, device):
        c = remote(src, xg.at[slot], xs.at[len(copies)], xr.at[slot], device)
        copies.append(c)
        c.start()

    def got(slot):
        remote(xg.at[slot], xg.at[slot], xs.at[0], xr.at[slot], (d, b, hc)).wait_recv()

    zto = [lax.rem(b + k, nb) for k in range(1, nb)]
    zfrom = [lax.rem(b + nb - k, nb) for k in range(1, nb)]
    for p in zto:
        put(x_ref, s, (d, p, h))
    put(x_ref, s, (d, b, hy))
    put(x_ref, s, (d, b, hc))
    for_slices(lambda dd, n: send_slice(dd, n).start())
    xg[s] = x_ref[...]

    @pl.when(active)
    def _():
        slices_in[me] = slices[hd]

    for f in zfrom:
        slot = xslot(f, h)
        got(slot)
        put(xg.at[slot], slot, (d, b, hy))
        put(xg.at[slot], slot, (d, b, hc))
    for f in [b] + zfrom:
        slot = xslot(f, hy)
        got(slot)
        put(xg.at[slot], slot, (d, b, hc))

    cut = 2 * D
    part_a = Spread(
        z, w_own.at[:, pl.ds(0, cut)], wg_ref, was, war, True, pl.ds(0, cut)
    )
    part_b = Spread(
        z, w_own.at[:, pl.ds(cut, 2 * D + LANES)], wg_ref, wbs, wbr, False,
        pl.ds(cut, 2 * D + LANES),
    )
    spread_steps = [
        step
        for pair in itertools.zip_longest(part_b.steps(), part_a.steps())
        for step in pair
        if step is not None
    ]

    def run_steps(count):
        for _ in range(min(count, len(spread_steps))):
            spread_steps.pop(0)()

    run_steps(2)

    @pl.when(active)
    def _():
        def got_slice(k, carry):
            t, device = any_peer(k)
            remote(slices_in.at[t], slices_in.at[t], ss.at[0], sr.at[t], device).wait_recv()
            return carry

        lax.fori_loop(1, nv, got_slice, 0)

    for f in [b] + zfrom:
        got(xslot(f, hc))
        got(xslot(f, hyc))

    rows = flatten_rows(slices_in[...])
    wh[:, : 2 * HS] = rows[:, : 2 * HS].astype(BF16)
    wh[:, :HS] = (rows[:, :HS] * HS ** (-0.5)).astype(BF16)
    wh[:, 2 * HS :] = rows[:, 2 * HS : 3 * HS].astype(BF16)
    gain = jnp.transpose(rows[:, LANES:])[HS : HS + 1, :]
    wanted = hd * BUCKETS + lax.broadcasted_iota(jnp.int32, (BUCKETS, D), 0)
    pick = (entry_ref[...] == wanted).astype(BF16)
    table = nn(pick, rows[:, LANES:].astype(BF16))[:, HS + 2 : HS + 3]
    bias_d[...] = bias_tile(table, 0)
    bias_s[...] = bias_tile(table, -BLOCK)
    far = table[BUCKETS // 2 - 1 : BUCKETS // 2, 0:1]
    per = BLOCK // PT
    half = BLOCK // 2

    def send_att(t):
        return remote(
            att_scr.at[t], att_out.at[hd], ats.at[t], atr.at[hd], (d, t // nh, t % nh)
        )

    for i in range(z.nq):
        run_steps(5)

        @pl.when(active)
        def _():
            here = slice(i * BLOCK, (i + 1) * BLOCK)
            x = xg[i * per : (i + 1) * per].reshape(BLOCK, D).astype(F32)
            inverse = lax.rsqrt(jnp.mean(x * x, axis=-1, keepdims=True) + EPSILON)
            low = (x * inverse * gain).astype(BF16)
            normed[here, :] = low
            mixed = nn(low, wh[...])
            qkv[here, :] = mixed.astype(BF16)
            v_t[:, here] = jnp.transpose(mixed[:, 2 * HS :]).astype(BF16)
            q = qkv[here, :HS]
            top = jnp.full((8, BLOCK), -1e30, F32)
            for j in range(i + 1):
                for u in range(2):
                    at = slice(j * BLOCK + u * half, j * BLOCK + (u + 1) * half)
                    part = slice(u * half, (u + 1) * half)
                    if j == i:
                        bias = bias_d[part, :]
                    elif j == i - 1:
                        bias = bias_s[part, :]
                    else:
                        bias = far
                    sc = nt(qkv[at, HS : 2 * HS], q) + bias
                    s_scr[at, :] = sc
                    top = jnp.maximum(top, jnp.max(sc.reshape(half // 8, 8, BLOCK), axis=0))
            top = jnp.max(top, axis=0, keepdims=True)
            total = jnp.zeros((8, BLOCK), F32)
            acc = jnp.zeros((HS, BLOCK), F32)
            for j in range(i + 1):
                for u in range(2):
                    at = slice(j * BLOCK + u * half, j * BLOCK + (u + 1) * half)
                    e = jnp.exp(s_scr[at, :] - top)
                    total = total + jnp.sum(e.reshape(half // 8, 8, BLOCK), axis=0)
                    p_scr[i, at, :] = e.astype(BF16)
                at = slice(j * BLOCK, (j + 1) * BLOCK)
                acc = acc + nn(v_t[:, at], p_scr[i, at, :])
            total = jnp.sum(total, axis=0, keepdims=True)
            both = jnp.concatenate([acc, jnp.broadcast_to(total, (HS, BLOCK))], axis=0)
            both = jnp.transpose(both)
            inv = 1.0 / both[:, HS:]
            att = (both[:, :HS] * inv).astype(BF16)
            attl[here, :] = jnp.concatenate([att.astype(F32), inv], axis=1)
            att_scr[i * per : (i + 1) * per] = att.reshape(per, PT, HS)
            to = slice(0, (i + 1) * BLOCK)
            pltpu.make_async_copy(p_scr.at[i, to], p_ref.at[i, to], loc.at[4 + i]).start()
            for u in range(per):
                t = i * per + u

                @pl.when(t != s)
                def _():
                    send_att(t).start()

                @pl.when(t == s)
                def _():
                    att_out[hd] = att_scr[t]

    @pl.when(active)
    def _():
        pltpu.make_async_copy(normed, normed_ref, loc.at[1]).start()
        pltpu.make_async_copy(qkv, qkv_ref, loc.at[2]).start()
        pltpu.make_async_copy(attl, attl_ref, loc.at[3]).start()

    run_steps(len(spread_steps))
    for n in range(HEAD_COUNT):

        @pl.when(jnp.logical_not(active & (hd == n)))
        def _():
            remote(
                att_out.at[n], att_out.at[n], ats.at[0], atr.at[n], (d, n // z.hb, n % z.hb)
            ).wait_recv()

    part_a.finish()
    part_b.finish()
    save_w.wait()
    for c in copies:
        c.wait_send()
    for_slices(lambda dd, n: send_slice(dd, n).wait_send())

    @pl.when(active)
    def _():
        pltpu.make_async_copy(normed, normed_ref, loc.at[1]).wait()
        pltpu.make_async_copy(qkv, qkv_ref, loc.at[2]).wait()
        pltpu.make_async_copy(attl, attl_ref, loc.at[3]).wait()
        for i in range(z.nq):
            to = slice(0, (i + 1) * BLOCK)
            pltpu.make_async_copy(p_scr.at[i, to], p_ref.at[i, to], loc.at[4 + i]).wait()
        for t in range(ns):

            @pl.when(t != s)
            def _():
                send_att(t).wait_send()


def attention_forward(z, entries, x, weights, router, rows, rel):
    D, S, HS, R, PT = z.D, z.S, HEAD_SIZE, z.R, z.PT
    nb = z.n_blk
    dma = pltpu.SemaphoreType.DMA
    vmem = pl.BlockSpec(memory_space=pltpu.VMEM)
    hbm = pl.BlockSpec(memory_space=pl.ANY)
    wide = 4 * D + LANES
    return pl.pallas_call(
        functools.partial(forward_kernel, z),
        out_shape=(
            jax.ShapeDtypeStruct((z.ndev, R, wide), BF16),
            jax.ShapeDtypeStruct((S, D), BF16),
            jax.ShapeDtypeStruct((S, 3 * HS), BF16),
            jax.ShapeDtypeStruct((z.nq, S, BLOCK), BF16),
            jax.ShapeDtypeStruct((S, 2 * HS), F32),
            jax.ShapeDtypeStruct((HEAD_COUNT, PT, HS), BF16),
        ),
        in_specs=[vmem] * 9,
        out_specs=(hbm, hbm, hbm, hbm, hbm, vmem),
        scratch_shapes=[
            pltpu.VMEM((R, wide), BF16),
            pltpu.VMEM((HEAD_COUNT, R, 4 * HS), BF16),
            pltpu.VMEM((z.ndev, R, 4 * HS), BF16),
            pltpu.VMEM((z.ns, PT, D), BF16),
            pltpu.VMEM((D, 3 * HS), BF16),
            pltpu.VMEM((BLOCK, BLOCK), F32),
            pltpu.VMEM((BLOCK, BLOCK), F32),
            pltpu.VMEM((S, D), BF16),
            pltpu.VMEM((S, 3 * HS), BF16),
            pltpu.VMEM((HS, S), BF16),
            pltpu.VMEM((S, BLOCK), F32),
            pltpu.VMEM((z.nq, S, BLOCK), BF16),
            pltpu.VMEM((S, 2 * HS), F32),
            pltpu.VMEM((z.ns, PT, HS), BF16),
            dma((nb - 1 + 2 + 2 * (nb - 1) + nb,)),
            dma((z.ns,)),
            dma((z.n_dp * HEAD_COUNT,)),
            dma((z.ndev,)),
            dma((spread_copies(z, True),)),
            dma((z.ndev,)),
            dma((spread_copies(z, False),)),
            dma((z.ndev,)),
            dma((z.ns,)),
            dma((HEAD_COUNT,)),
            dma((4 + z.nq,)),
        ],
        compiler_params=pltpu.CompilerParams(
            collective_id=0, has_side_effects=True, vmem_limit_bytes=48 * 1024 * 1024
        ),
        name="attention_forward",
    )(entries, x, *weights, router, rows, rel)


def middle_kernel(
    z, att_in, x_ref, w_ref, order_ref, ids_ref, win_ref, wout_ref, cot_ref,
    layer_ref, gmid_ref, gatt_ref, dwo_ref, all_ref,
    win, wout, wo3, misc3, disp, exp_in, ret, back, route, att_cat, pre_scr, out_acc, gg_acc,
    loc, dis_s, dis_r, ret_s, ret_r, all_s, all_r,
):
    d, b, h = place()
    nb, nh, nd, ns = z.n_blk, z.n_head, z.n_dp, z.ns
    D, E, PT, NG, C8 = z.D, z.E, z.PT, z.NG, z.cap8
    me = d * ns + b * nh + h
    g = d * nb + b
    hy = lax.rem(h + 2, nh)
    hc = h + 1 - 2 * lax.rem(h, 2)
    hyc = lax.rem(hc + 2, nh)

    def exp_peer(k):
        e = lax.rem(g + k, NG)
        return e, (e // nb, lax.rem(e, nb), h)

    def exp_from(k):
        e = lax.rem(g + NG - k, NG)
        return e, (e // nb, lax.rem(e, nb), h)

    for k in range(1, NG):
        signal(exp_peer(k)[1])
    signal((d, b, hy))
    signal((d, b, hc))
    local = [
        pltpu.make_async_copy(w_ref.at[:, :, pl.ds(3 * D, D)], wo3, loc.at[0]),
        pltpu.make_async_copy(w_ref.at[:, :, pl.ds(4 * D, LANES)], misc3, loc.at[1]),
        pltpu.make_async_copy(win_ref.at[0], win, loc.at[2]),
        pltpu.make_async_copy(wout_ref.at[0], wout, loc.at[3]),
    ]
    for c in local:
        c.start()

    ids_row = ids_ref[pl.ds(me, 1), :]
    order_row = order_ref[...]
    ids_col = jnp.transpose(jnp.broadcast_to(ids_row, (PT, PT)))
    order_col = jnp.transpose(jnp.broadcast_to(order_row, (PT, PT)))
    earlier = (order_col < order_row) & (ids_col == ids_row)
    rank = jnp.sum(earlier.astype(jnp.int32), axis=0, keepdims=True)
    slot = lax.broadcasted_iota(jnp.int32, (C8, PT), 0)
    base = (rank == slot) & (slot < z.cap)
    lane = lax.broadcasted_iota(jnp.int32, (1, LANES), 1)
    share = jnp.zeros((1, LANES), F32)
    ids_all = ids_ref[...]
    for e in range(E):
        route[e * C8 : (e + 1) * C8, :] = (base & (ids_row == e)).astype(F32)
        count = jnp.sum((ids_all == e).astype(F32), axis=1, keepdims=True)
        count = jnp.sum(count, axis=0, keepdims=True)
        share = share + jnp.where(lane == e, count, 0.0)
    share = share * (AUX_WEIGHT * E / (ids_all.shape[0] * ids_all.shape[1]))
    chosen = ids_col[:, :1] == lane
    picks = route[...].astype(BF16)

    x = x_ref[...].astype(F32)
    cot = cot_ref[...].astype(F32)
    for n in range(HEAD_COUNT):
        att_cat[:, n * HEAD_SIZE : (n + 1) * HEAD_SIZE] = att_in[n]
    att = att_cat[...]
    local[0].wait()
    local[1].wait()
    wo = flatten_rows(wo3[...]).astype(BF16)
    misc = flatten_rows(misc3[...])
    router = misc.astype(BF16)
    gain = jnp.transpose(misc)[E + 1 : E + 2, :]
    middle = x + nn(att, wo)
    inverse = lax.rsqrt(jnp.mean(middle * middle, axis=-1, keepdims=True) + EPSILON)
    routed = (middle * inverse * gain).astype(BF16)
    await_barrier(NG - 1 + 2)

    def send_disp(part, k):
        e, device = exp_peer(k)
        at = part * NG
        return remote(
            disp.at[part, e], exp_in.at[part, g], dis_s.at[at + k], dis_r.at[at + g], device
        )

    def dispatch(part, values):
        disp[part] = nn(picks, values).reshape(E, C8, D).astype(BF16)
        for k in range(1, NG):
            send_disp(part, k).start()
        exp_in[part, g] = disp[part, g]

    def arrivals(part):
        for k in range(1, NG):
            e, device = exp_from(k)
            ref = exp_in.at[part, e]
            remote(ref, ref, dis_s.at[0], dis_r.at[part * NG + e], device).wait_recv()

    def send_ret(part, k):
        e, device = exp_peer(k)
        at = part * NG
        return remote(
            ret.at[part, e], back.at[part, g], ret_s.at[at + k], ret_r.at[at + g], device
        )

    def give_back(part, values):
        ret[part] = values.reshape(NG, C8, D).astype(BF16)
        for k in range(1, NG):
            send_ret(part, k).start()
        back[part, g] = ret[part, g]

    def returns(part):
        for k in range(1, NG):
            e, device = exp_from(k)
            ref = back.at[part, e]
            remote(ref, ref, ret_s.at[0], ret_r.at[part * NG + e], device).wait_recv()
        rows = back[part].astype(F32).reshape(E * C8, D).astype(BF16)
        return tn(picks, rows)

    def share_slots(part):
        at = 3 * part
        out = [
            remote(
                exp_in.at[part], all_ref.at[part, h], all_s.at[at], all_r.at[part * nh + h],
                (d, b, hy),
            ),
            remote(
                exp_in.at[part], all_ref.at[part, h], all_s.at[at + 1], all_r.at[part * nh + h],
                (d, b, hc),
            ),
            pltpu.make_async_copy(exp_in.at[part], all_ref.at[part, h], loc.at[4 + part]),
        ]
        for c in out:
            c.start()
        return out

    def got_slots(part, hh):
        ref = all_ref.at[part, hh]
        remote(ref, ref, all_s.at[0], all_r.at[part * nh + hh], (d, b, hc)).wait_recv()

    def pass_slots(part):
        got_slots(part, hy)
        ref = all_ref.at[part, hy]
        c = remote(ref, ref, all_s.at[3 * part + 2], all_r.at[part * nh + hy], (d, b, hc))
        c.start()
        return c

    dispatch(0, routed)
    logits = jnp.where(lane < E, nn(routed, router), -1e30)
    exps = jnp.exp(logits - jnp.max(logits, axis=-1, keepdims=True))
    probs = exps / jnp.sum(exps, axis=-1, keepdims=True)
    gate = jnp.sum(jnp.where(chosen, probs, 0.0), axis=-1, keepdims=True)
    dispatch(1, (gate * cot).astype(BF16))
    local[2].wait()
    local[3].wait()
    chunk = D
    chunks = z.FF // chunk

    arrivals(0)
    rows_in = exp_in[0].astype(F32).reshape(NG * C8, D).astype(BF16)
    out_acc[...] = jnp.zeros_like(out_acc)

    def forward_step(c, carry):
        at = pl.ds(pl.multiple_of(c * chunk, chunk), chunk)
        pre = nn(rows_in, win[:, at])
        pre_scr[:, at] = pre
        phi, _ = normal_parts(pre)
        out_acc[...] += nn((pre * phi).astype(BF16), wout[at, :])
        return carry

    lax.fori_loop(0, chunks, forward_step, 0)
    give_back(0, out_acc[...])

    arrivals(1)
    grad_out = exp_in[1].astype(F32).reshape(NG * C8, D).astype(BF16)
    gg_acc[...] = jnp.zeros_like(gg_acc)

    def backward_step(c, carry):
        at = pl.ds(pl.multiple_of(c * chunk, chunk), chunk)
        pre = pre_scr[:, at]
        phi, bell = normal_parts(pre)
        gh = nt(grad_out, wout[at, :]).astype(BF16).astype(F32)
        gp = (gh * (phi + pre * bell * INV_ROOT_TWO_PI)).astype(BF16)
        gg_acc[...] += nt(gp, win[:, at])
        return carry

    lax.fori_loop(0, chunks, backward_step, 0)
    give_back(1, gg_acc[...])
    moved = share_slots(0) + share_slots(1)

    expert_rows = returns(0)
    layer_ref[...] = (middle + gate * expert_rows).astype(BF16)
    grad_gate = jnp.sum(cot * expert_rows, axis=-1, keepdims=True)
    grad_probs = jnp.where(chosen, grad_gate, 0.0) + share
    inner = jnp.sum(probs * grad_probs, axis=-1, keepdims=True)
    grad_logits = (probs * (grad_probs - inner)).astype(BF16)
    from_router = nt(grad_logits, router)
    grad_routed = returns(1) + from_router
    scaled = grad_routed * gain
    mean = jnp.mean(scaled * middle, axis=-1, keepdims=True)
    gmid = cot + inverse * scaled - middle * (inverse * inverse * inverse) * mean
    gmid_ref[...] = gmid
    low_mid = gmid.astype(BF16)
    gatt = nt(low_mid, wo).astype(BF16)
    for n in range(HEAD_COUNT):
        gatt_ref[n] = gatt[:, n * HEAD_SIZE : (n + 1) * HEAD_SIZE]
    term = grad_routed * middle * inverse
    high = term.astype(BF16)
    rest = (term - high.astype(F32)).astype(BF16)
    ones = jnp.broadcast_to((lane == E).astype(BF16), (PT, LANES))
    small = tn(routed, grad_logits) + tn(high, ones) + tn(rest, ones)
    terms = jnp.concatenate([tn(att, low_mid), small], axis=1)
    for t in range(z.ndev):
        dwo_ref[t % nh, t // nh] = terms[t * z.R : (t + 1) * z.R].astype(BF16)

    passed = [pass_slots(0), pass_slots(1)]
    for part in range(2):
        for hh in (hc, hyc):
            got_slots(part, hh)
    for n, c in enumerate(moved):
        if n % 3 == 2:
            c.wait()
        else:
            c.wait_send()
    for c in passed:
        c.wait_send()
    for part in range(2):
        for k in range(1, NG):
            send_disp(part, k).wait_send()
            send_ret(part, k).wait_send()


def middle_part(z, att, x, wg, order, ids, w_in, w_out, cot):
    D, PT, NG, E, C8 = z.D, z.PT, z.NG, z.E, z.cap8
    dma = pltpu.SemaphoreType.DMA
    vmem = pl.BlockSpec(memory_space=pltpu.VMEM)
    hbm = pl.BlockSpec(memory_space=pl.ANY)
    return pl.pallas_call(
        functools.partial(middle_kernel, z),
        out_shape=(
            jax.ShapeDtypeStruct((PT, D), BF16),
            jax.ShapeDtypeStruct((PT, D), F32),
            jax.ShapeDtypeStruct((HEAD_COUNT, PT, HEAD_SIZE), BF16),
            jax.ShapeDtypeStruct((z.n_head, NG, z.R, D + LANES), BF16),
            jax.ShapeDtypeStruct((2, z.n_head, NG, C8, D), BF16),
        ),
        in_specs=[vmem, vmem, hbm, vmem, vmem, hbm, hbm, vmem],
        out_specs=(vmem, vmem, vmem, vmem, hbm),
        scratch_shapes=[
            pltpu.VMEM((D, z.FF), BF16),
            pltpu.VMEM((z.FF, D), BF16),
            pltpu.VMEM((z.ndev, z.R, D), BF16),
            pltpu.VMEM((z.ndev, z.R, LANES), BF16),
            pltpu.VMEM((2, E, C8, D), BF16),
            pltpu.VMEM((2, NG, C8, D), BF16),
            pltpu.VMEM((2, NG, C8, D), BF16),
            pltpu.VMEM((2, E, C8, D), BF16),
            pltpu.VMEM((E * C8, PT), F32),
            pltpu.VMEM((PT, D), BF16),
            pltpu.VMEM((NG * C8, z.FF), F32),
            pltpu.VMEM((NG * C8, D), F32),
            pltpu.VMEM((NG * C8, D), F32),
            dma((6,)),
            dma((2 * NG,)),
            dma((2 * NG,)),
            dma((2 * NG,)),
            dma((2 * NG,)),
            dma((6,)),
            dma((2 * z.n_head,)),
        ],
        compiler_params=pltpu.CompilerParams(
            collective_id=1, has_side_effects=True, vmem_limit_bytes=56 * 1024 * 1024
        ),
        name="experts_and_norms",
    )(att, x, wg, order, ids, w_in, w_out, cot)


def backward_kernel(
    z, gatt_ref, dwo_ref, normed_ref, qkv_ref, p_ref, attl_ref, wg_ref,
    wq_ref, wk_ref, wv_ref, x_ref, gmid_ref,
    gtok_ref, gain1_ref, gq_ref, gk_ref, gv_ref, go_ref, table_ref, gain2_ref, router_ref,
    w3, wfull, misc3, normed, qkv, probs, attl, k_t, do_in, grad_cat, dkv, dqkv, dw, dw3,
    diag, sub, far, dq_in, dw_in, first_in, second_src, second_in,
    loc, do_s, do_r, dq_s, dq_r, dw_s, dw_r, r1_s, r1_r, r2_s, r2_r,
):
    d, b, h = place()
    nb, nh, nd, ns, nv, NG = z.n_blk, z.n_head, z.n_dp, z.ns, z.ndev, z.NG
    D, R, PT, HS, E = z.D, z.R, z.PT, HEAD_SIZE, z.E
    s = b * nh + h
    me = d * ns + s
    g = d * nb + b
    hd = b * z.hb + jnp.minimum(h, z.hb - 1)
    active = h < z.hb

    def any_peer(k):
        t = lax.rem(me + k, nv)
        return t, (t // ns, lax.rem(t // nh, nb), lax.rem(t, nh))

    def greet(k, carry):
        signal(any_peer(k)[1])
        return carry

    lax.fori_loop(1, nv, greet, 0)
    local = [
        pltpu.make_async_copy(qkv_ref, qkv, loc.at[0]),
        pltpu.make_async_copy(attl_ref, attl, loc.at[1]),
        pltpu.make_async_copy(p_ref, probs, loc.at[2]),
        pltpu.make_async_copy(normed_ref, normed, loc.at[3]),
        pltpu.make_async_copy(wg_ref.at[:, :, pl.ds(0, 3 * D)], w3, loc.at[4]),
        pltpu.make_async_copy(wg_ref.at[:, :, pl.ds(4 * D, LANES)], misc3, loc.at[5]),
    ]
    for c in local:
        c.start()
    await_barrier(nv - 1)

    def send_do(n):
        hb, hh = n // z.hb, n % z.hb
        return remote(gatt_ref.at[n], do_in.at[s], do_s.at[n], do_r.at[s], (d, hb, hh))

    for n in range(HEAD_COUNT):
        mine = active & (hd == n)

        @pl.when(jnp.logical_not(mine))
        def _():
            send_do(n).start()

        @pl.when(mine)
        def _():
            do_in[s] = gatt_ref[n]

    def send_first(k):
        hh = lax.rem(h + k, nh)
        return remote(dwo_ref.at[hh], first_in.at[h], r1_s.at[k], r1_r.at[h], (d, b, hh))

    def group_peer(k):
        e = lax.rem(g + k, NG)
        return e, (e // nb, lax.rem(e, nb), h)

    def send_second(k):
        e, device = group_peer(k)
        return remote(second_src.at[e], second_in.at[g], r2_s.at[k], r2_r.at[g], device)

    for k in range(1, nh):
        send_first(k).start()
    first_in[h] = dwo_ref[h]

    def second_stage():
        for k in range(1, nh):
            hh = lax.rem(h + k, nh)
            remote(
                first_in.at[hh], first_in.at[hh], r1_s.at[0], r1_r.at[hh], (d, b, hh)
            ).wait_recv()

        def group_sum(e, carry):
            acc = first_in[0, e].astype(F32)
            for hh in range(1, nh):
                acc = acc + first_in[hh, e].astype(F32)
            second_src[e] = acc.astype(BF16)
            return carry

        lax.fori_loop(0, NG, group_sum, 0)
        for k in range(1, NG):
            send_second(k).start()
        second_in[g] = second_src[g]

    for c in local:
        c.wait()
    wfull[...] = flatten_rows(w3[...]).astype(BF16)
    gain = jnp.transpose(flatten_rows(misc3[...]))[E : E + 1, :]

    def send_dq(t):
        return remote(dqkv.at[t], dq_in.at[hd], dq_s.at[t], dq_r.at[hd], (d, t // nh, t % nh))

    def send_dw(k):
        t, device = any_peer(k)
        slot = d * HEAD_COUNT + hd
        return remote(dw3.at[t], dw_in.at[slot], dw_s.at[k], dw_r.at[slot], device)

    per = BLOCK // PT
    part_rows = BLOCK // 2

    @pl.when(active)
    def _():
        for j in range(z.nq):
            at = slice(j * BLOCK, (j + 1) * BLOCK)
            k_t[:, at] = jnp.transpose(qkv[at, HS : 2 * HS].astype(F32)).astype(BF16)
        dkv[...] = jnp.zeros_like(dkv)
        dw[...] = jnp.zeros_like(dw)
        diag[...] = jnp.zeros_like(diag)
        sub[...] = jnp.zeros_like(sub)
        far[...] = jnp.zeros_like(far)

        def got_do(k, carry):
            t = lax.rem(s + k, ns)
            remote(
                do_in.at[t], do_in.at[t], do_s.at[0], do_r.at[t],
                (d, t // nh, lax.rem(t, nh)),
            ).wait_recv()
            return carry

        lax.fori_loop(1, ns, got_do, 0)

    for i in reversed(range(z.nq)):
        if i == z.nq // 2:
            second_stage()

        @pl.when(active)
        def _():
            here = slice(i * BLOCK, (i + 1) * BLOCK)
            att = attl[here, :HS]
            inv = attl[here, HS:]
            do = do_in[i * per : (i + 1) * per].reshape(BLOCK, HS).astype(F32)
            do = (do * inv).astype(BF16)
            prod = do.astype(F32) * att
            high = prod.astype(BF16)
            rest = (prod - high.astype(F32)).astype(BF16)
            ones = jnp.ones((8, HS), BF16)
            delta = (nt(ones, high) + nt(ones, rest))[0:1, :]
            q = qkv[here, :HS]
            dq_t = jnp.zeros((HS, BLOCK), F32)
            for j in range(i + 1):
                for u in range(2):
                    at = slice(j * BLOCK + u * part_rows, j * BLOCK + (u + 1) * part_rows)
                    p = probs[i, at, :]
                    ds = p.astype(F32) * (nt(qkv[at, 2 * HS :], do) - delta)
                    low = ds.astype(BF16)
                    both = jnp.concatenate([nn(low, q), nn(p, do)], axis=1)
                    if j == i:
                        dkv[at, :] = both if i == z.nq - 1 else dkv[at, :] + both
                        diag[u * part_rows : (u + 1) * part_rows, :] += low.astype(F32)
                    else:
                        dkv[at, :] += both
                        if j == i - 1:
                            sub[u * part_rows : (u + 1) * part_rows, :] += low.astype(F32)
                        else:
                            far[...] += jnp.sum(
                                low.astype(F32).reshape(part_rows // 8, 8, BLOCK), axis=0
                            )
                    dq_t = dq_t + nn(k_t[:, at], low)
            dq = jnp.transpose(dq_t) * HS ** (-0.5)
            parts = jnp.concatenate([dq, dkv[here, :]], axis=1).astype(BF16)
            dw[...] += tn(normed[here, :], parts)
            dqkv[i * per : (i + 1) * per] = parts.reshape(per, PT, 3 * HS)
            for u in range(per):
                t = i * per + u

                @pl.when(t != s)
                def _():
                    send_dq(t).start()

                @pl.when(t == s)
                def _():
                    dq_in[hd] = dqkv[t]

    @pl.when(active)
    def _():
        jj = lax.broadcasted_iota(jnp.int32, (BLOCK, BLOCK), 0)
        ii = lax.broadcasted_iota(jnp.int32, (BLOCK, BLOCK), 1)
        lane = lax.broadcasted_iota(jnp.int32, (1, HS), 1)
        sums = jnp.zeros((1, HS), F32)
        half = BUCKETS // 2
        bounds = (0,) + LIMITS + (1 << 30,)
        tile_d, tile_s = diag[...], sub[...]

        def total(values):
            return jnp.sum(jnp.sum(values, axis=0, keepdims=True), axis=1, keepdims=True)

        for n in range(half):
            lo, hi = bounds[n], bounds[n + 1]
            dist = ii - jj
            part = total(
                jnp.where((dist >= lo) & (dist < hi), tile_d, 0.0)
                + jnp.where((dist + BLOCK >= lo) & (dist + BLOCK < hi), tile_s, 0.0)
            )
            if n == half - 1:
                part = part + total(far[...])
            sums = sums + jnp.where(lane == n, part, 0.0)
            if n > 0:
                part = total(jnp.where((-dist >= lo) & (-dist < hi), tile_d, 0.0))
                sums = sums + jnp.where(lane == half + n, part, 0.0)
        wide = jnp.concatenate([dw[...], jnp.broadcast_to(sums, (D, HS))], axis=1)
        split_rows(dw3, wide, R)

        def start_dw(k, carry):
            send_dw(k).start()
            return carry

        lax.fori_loop(1, nv, start_dw, 0)
        dw_in[d * HEAD_COUNT + hd] = dw3[me]

    for k in range(1, NG):
        e, device = group_peer(k)
        remote(second_in.at[e], second_in.at[e], r2_s.at[0], r2_r.at[e], device).wait_recv()
    acc = lax.fori_loop(
        0, NG, lambda t, a: a + second_in[t].astype(F32), jnp.zeros((R, D + LANES), F32)
    )
    go_ref[...] = acc[:, :D]
    router_ref[...] = acc[:, D : D + E]
    gain2_ref[...] = acc[:, D + E : D + E + 1]

    for n in range(HEAD_COUNT):

        @pl.when(jnp.logical_not(active & (hd == n)))
        def _():
            remote(
                dq_in.at[n], dq_in.at[n], dq_s.at[0], dq_r.at[n], (d, n // z.hb, n % z.hb)
            ).wait_recv()

        part = dq_in[n]
        for m in range(3):
            grad_cat[:, m * D + n * HS : m * D + (n + 1) * HS] = part[:, m * HS : (m + 1) * HS]
    grad_normed = nt(grad_cat[...], wfull[...])
    x = x_ref[...].astype(F32)
    inverse = lax.rsqrt(jnp.mean(x * x, axis=-1, keepdims=True) + EPSILON)
    scaled = grad_normed * gain
    mean = jnp.mean(scaled * x, axis=-1, keepdims=True)
    grad_in = inverse * scaled - x * (inverse * inverse * inverse) * mean
    gtok_ref[...] = (gmid_ref[...] + grad_in).astype(BF16)

    for dd in range(nd):
        for n in range(HEAD_COUNT):

            @pl.when(jnp.logical_not(active & (hd == n) & (d == dd)))
            def _():
                slot = dd * HEAD_COUNT + n
                remote(
                    dw_in.at[slot], dw_in.at[slot], dw_s.at[0], dw_r.at[slot],
                    (dd, n // z.hb, n % z.hb),
                ).wait_recv()

    lane = lax.broadcasted_iota(jnp.int32, (1, BUCKETS), 1)
    slot_lane = lax.broadcasted_iota(jnp.int32, (1, z.RL), 1)
    own_table = jnp.zeros((1, z.RL), F32)
    first = jnp.zeros((R, 1), F32)
    for n in range(HEAD_COUNT):
        part = dw_in[n].astype(F32)
        for dd in range(1, nd):
            part = part + dw_in[dd * HEAD_COUNT + n].astype(F32)
        at = slice(n * HS, (n + 1) * HS)
        for m, (out, w) in enumerate(((gq_ref, wq_ref), (gk_ref, wk_ref), (gv_ref, wv_ref))):
            cols = part[:, m * HS : (m + 1) * HS]
            out[:, at] = cols
            first = first + jnp.sum(cols * w[:, at].astype(F32), axis=-1, keepdims=True)
        line = part[0:1, 3 * HS : 3 * HS + BUCKETS]
        for k in range(z.RL):
            hit = lane + n * BUCKETS == me * z.RL + k
            value = jnp.sum(jnp.where(hit, line, 0.0), axis=1, keepdims=True)
            own_table = own_table + jnp.where(slot_lane == k, value, 0.0)
    own_gain = misc3[pl.ds(me, 1)].astype(F32).reshape(R, LANES)[:, E : E + 1]
    gain1_ref[...] = first / own_gain
    table_ref[...] = own_table

    for k in range(1, nh):
        send_first(k).wait_send()
    for k in range(1, NG):
        send_second(k).wait_send()
    for n in range(HEAD_COUNT):

        @pl.when(jnp.logical_not(active & (hd == n)))
        def _():
            send_do(n).wait_send()

    @pl.when(active)
    def _():
        for t in range(ns):

            @pl.when(t != s)
            def _():
                send_dq(t).wait_send()

        def sent_dw(k, carry):
            send_dw(k).wait_send()
            return carry

        lax.fori_loop(1, nv, sent_dw, 0)


def attention_backward(z, gatt, dwo, normed, qkv, probs, attl, wg, weights, x, gmid):
    D, R, PT, S, HS, E, NG = z.D, z.R, z.PT, z.S, HEAD_SIZE, z.E, z.NG
    dma = pltpu.SemaphoreType.DMA
    vmem = pl.BlockSpec(memory_space=pltpu.VMEM)
    hbm = pl.BlockSpec(memory_space=pl.ANY)
    return pl.pallas_call(
        functools.partial(backward_kernel, z),
        out_shape=(
            jax.ShapeDtypeStruct((PT, D), BF16),
            jax.ShapeDtypeStruct((R, 1), F32),
            jax.ShapeDtypeStruct((R, D), F32),
            jax.ShapeDtypeStruct((R, D), F32),
            jax.ShapeDtypeStruct((R, D), F32),
            jax.ShapeDtypeStruct((R, D), F32),
            jax.ShapeDtypeStruct((1, z.RL), F32),
            jax.ShapeDtypeStruct((R, 1), F32),
            jax.ShapeDtypeStruct((R, E), F32),
        ),
        in_specs=[vmem, vmem, hbm, hbm, hbm, hbm, hbm, vmem, vmem, vmem, vmem, vmem],
        out_specs=(vmem,) * 9,
        scratch_shapes=[
            pltpu.VMEM((z.ndev, R, 3 * D), BF16),
            pltpu.VMEM((D, 3 * D), BF16),
            pltpu.VMEM((z.ndev, R, LANES), BF16),
            pltpu.VMEM((S, D), BF16),
            pltpu.VMEM((S, 3 * HS), BF16),
            pltpu.VMEM((z.nq, S, BLOCK), BF16),
            pltpu.VMEM((S, 2 * HS), F32),
            pltpu.VMEM((HS, S), BF16),
            pltpu.VMEM((z.ns, PT, HS), BF16),
            pltpu.VMEM((PT, 3 * D), BF16),
            pltpu.VMEM((S, 2 * HS), F32),
            pltpu.VMEM((z.ns, PT, 3 * HS), BF16),
            pltpu.VMEM((D, 3 * HS), F32),
            pltpu.VMEM((z.ndev, R, 4 * HS), BF16),
            pltpu.VMEM((BLOCK, BLOCK), F32),
            pltpu.VMEM((BLOCK, BLOCK), F32),
            pltpu.VMEM((8, BLOCK), F32),
            pltpu.VMEM((HEAD_COUNT, PT, 3 * HS), BF16),
            pltpu.VMEM((z.n_dp * HEAD_COUNT, R, 4 * HS), BF16),
            pltpu.VMEM((z.n_head, NG, R, D + LANES), BF16),
            pltpu.VMEM((NG, R, D + LANES), BF16),
            pltpu.VMEM((NG, R, D + LANES), BF16),
            dma((6,)),
            dma((HEAD_COUNT,)),
            dma((z.ns,)),
            dma((z.ns,)),
            dma((HEAD_COUNT,)),
            dma((z.ndev,)),
            dma((z.n_dp * HEAD_COUNT,)),
            dma((z.n_head,)),
            dma((z.n_head,)),
            dma((NG,)),
            dma((NG,)),
        ],
        compiler_params=pltpu.CompilerParams(
            collective_id=2, has_side_effects=True, vmem_limit_bytes=58 * 1024 * 1024
        ),
        name="attention_backward",
    )(gatt, dwo, normed, qkv, probs, attl, wg, *weights, x, gmid)


def expert_kernel(z, slots_ref, win_ref, wout_ref, gin_ref, gout_ref, rows_in, rows_t, grad_out):
    @pl.when(pl.program_id(0) == 0)
    def _():
        for n in range(z.n_head):
            count = z.NG * z.cap8
            at = slice(n * count, (n + 1) * count)
            rows_in[at, :] = slots_ref[0, n].astype(F32).reshape(count, z.D).astype(BF16)
            grad_out[at, :] = slots_ref[1, n].astype(F32).reshape(count, z.D).astype(BF16)
        rows_t[...] = jnp.transpose(rows_in[...])

    w1 = win_ref[0]
    w2 = wout_ref[0]
    pre = nn(rows_in[...], w1)
    phi, bell = normal_parts(pre)
    hidden = (pre * phi).astype(BF16)
    gh = nt(grad_out[...], w2).astype(BF16).astype(F32)
    gp = (gh * (phi + pre * bell * INV_ROOT_TWO_PI)).astype(BF16)
    gin_ref[0] = nn(rows_t[...], gp)
    gout_ref[0] = tn(hidden, grad_out[...])


def expert_weights(z, slots, w_in, w_out):
    chunk = 512
    total = z.n_head * z.NG * z.cap8
    in_chunk = pl.BlockSpec((1, z.D, chunk), lambda i: (0, 0, i))
    out_chunk = pl.BlockSpec((1, chunk, z.D), lambda i: (0, i, 0))
    return pl.pallas_call(
        functools.partial(expert_kernel, z),
        grid=(z.FF // chunk,),
        out_shape=(
            jax.ShapeDtypeStruct((1, z.D, z.FF), F32),
            jax.ShapeDtypeStruct((1, z.FF, z.D), F32),
        ),
        in_specs=[pl.BlockSpec(memory_space=pltpu.VMEM), in_chunk, out_chunk],
        out_specs=(in_chunk, out_chunk),
        scratch_shapes=[
            pltpu.VMEM((total, z.D), BF16),
            pltpu.VMEM((z.D, total), BF16),
            pltpu.VMEM((total, z.D), BF16),
        ],
        compiler_params=pltpu.CompilerParams(
            dimension_semantics=("arbitrary",), vmem_limit_bytes=48 * 1024 * 1024
        ),
        name="expert_weight_grads",
    )(slots, w_in, w_out)


def local(
    sizes,
    tokens,
    order,
    expert_ids,
    norm1_gain,
    w_query,
    w_key,
    w_value,
    w_attn_out,
    rel_table,
    norm2_gain,
    w_router,
    w_in,
    w_out,
    cotangent,
):
    R, D = w_query.shape
    E = w_router.shape[1]
    z = Sizes(*sizes, R, D, E, w_in.shape[2], tokens.shape[1])
    rel = jnp.pad(rel_table, (0, R - rel_table.shape[0]))[None, :]
    gains = jnp.stack([norm1_gain, norm2_gain])
    row = np.arange(D)
    entries = np.where(row % R < z.RL, row // R * z.RL + row % R, -1).astype(np.int32)[None, :]
    ids = expert_ids.reshape(-1, z.PT)
    x = tokens.reshape(z.PT, D)
    cot = cotangent.reshape(z.PT, D)

    wg, normed, qkv, probs, attl, att = attention_forward(
        z,
        jnp.asarray(entries),
        x,
        (w_query, w_key, w_value, w_attn_out),
        w_router,
        gains.astype(F32),
        rel.astype(F32),
    )
    layer, gmid, gatt, dwo, slots = middle_part(z, att, x, wg, order, ids, w_in, w_out, cot)
    gtok, gain1, gq, gk, gv, go, table, gain2, router = attention_backward(
        z, gatt, dwo, normed, qkv, probs, attl, wg, (w_query, w_key, w_value), x, gmid
    )
    g_in, g_out = expert_weights(z, slots, w_in, w_out)
    return (
        layer.reshape(tokens.shape),
        gtok.reshape(tokens.shape),
        gain1.reshape(R),
        gq,
        gk,
        gv,
        go,
        table.reshape(z.RL),
        gain2.reshape(R),
        router,
        g_in,
        g_out,
    )


def solution(mesh):
    everywhere = ("dp", "blk", "head")
    rows, table = P(everywhere), P(everywhere, None)
    tokens = P("dp", ("blk", "head"), None)
    expert = P(("dp", "blk"), None, None)
    in_specs = (
        tokens,
        P("dp", ("blk", "head")),
        P(),
        rows,
        table,
        table,
        table,
        table,
        rows,
        rows,
        table,
        expert,
        expert,
        tokens,
    )
    out_specs = (
        tokens, tokens, rows, table, table, table, table, rows, rows, table, expert, expert
    )
    sizes = (mesh.shape["dp"], mesh.shape["blk"], mesh.shape["head"])
    return jax.shard_map(
        functools.partial(local, sizes),
        mesh=mesh,
        in_specs=in_specs,
        out_specs=out_specs,
        check_vma=False,
    )
```

time: 270 us -> 234 us (0.87)
  Pallas kernels: 249 us -> 213 us
    pallas_call x1, Pallas kernels: 58.5 us -> 44 us  [middle_part(): pl.pallas_call(functools.partial(middle_kernel, z), out_shape=(jax.ShapeD...]
    pallas_call x1, Pallas kernels: 81.5 us -> 69.5 us  [attention_backward(): pl.pallas_call(functools.partial(backward_kernel, z), out_shape=(jax.Shap...]
    pallas_call x2 -> x1, Pallas kernels: 86.1 us -> 76.5 us  [attention_forward(): pl.pallas_call(functools.partial(forward_kernel, z), out_shape=(jax.Shape...]
    unnamed x39 -> x45, local copies, waits for them, and re-layouts: 14.5 us -> 15.6 us
where the time goes in v2:
time: 234 us
  Pallas kernels  213 us (91%)
  local copies, waits for them, and re-layouts  15.6 us (7%)
  other arithmetic  4.01 us (2%)
    pallas_call x1, Pallas kernels, attention_forward(): pl.pallas_call(functools.partial(forward_kernel, z), out_shape=(jax.Shape...  76.5 us
    pallas_call x1, Pallas kernels, attention_backward(): pl.pallas_call(functools.partial(backward_kernel, z), out_shape=(jax.Shap...  69.5 us
    pallas_call x1, Pallas kernels, middle_part(): pl.pallas_call(functools.partial(middle_kernel, z), out_shape=(jax.ShapeD...  44 us
    pallas_call x1, Pallas kernels, expert_weights(): pl.pallas_call(functools.partial(expert_kernel, z), grid=(z.FF // chunk,)...  23.2 us
    unnamed x45, local copies, waits for them, and re-layouts  15.6 us

profile of v2, /device:TPU:0, one launch (start us, length us, event | category | flops | bytes accessed | tf_op | source)
XLA Modules:
  0.0 233.6 jit_solution(17202823002958017121)
XLA Ops:
  0.6 0.7 bitcast_convert_fusion.rel_ref
  1.3 0.7 maximum_convert_fusion.rows_ref
  2.0 0.8 copy.29.router_ref
  2.7 0.0 copy-start.2
  2.7 0.9 copy-done.2
  3.7 0.0 copy-start.6
  3.7 0.8 copy-done.6
  4.4 0.0 copy-start.7
  4.4 0.8 copy-done.7
  5.2 0.0 copy-start.8
  5.2 0.8 copy-done.8
  6.0 0.0 copy-start.9
  6.0 0.8 copy-done.9
  6.7 0.0 copy-start.10
  6.7 0.7 copy-done.10
  7.4 76.5 %attention_forward.1 = (bf16[32,24,3200]{2,1,0:T(8,128)(2,1)}, bf16[2048,768]{1,0:T(8,128)(2,1)S(1)}, bf16[2048,192]{1,0:T(8,128)(2,1)S(1)}, bf16[8,2048,256]{2,...) custom-call(s32[1,768]{1,0:T(1,128)S(1)} %copy-done.10, bf16[128,768]{1,0:T(8,128)(2,1)S(1)} %bitcast.13, ...), custom_call_target="tpu_custom_call" | custom-call | tf_op jit(solution)/shard_map/attention_forward/pallas_call | solution.py:472
  83.9 0.0 copy-start
  84.0 1.7 copy-done
  85.6 0.0 copy-start.3
  85.6 1.0 copy-done.3
  86.6 0.0 copy-start.4
  86.6 1.0 copy-done.4
  87.6 0.0 copy-start.5
  87.6 0.8 copy-done.5
  88.3 44.0 %experts_and_norms.1 = (bf16[128,768]{1,0:T(8,128)(2,1)}, f32[128,768]{1,0:T(8,128)}, bf16[12,128,64]{2,1,0:T(8,128)(2,1)}, bf16[4,8,24,896]{3,2,1,0:T(8,128)(2,1)}, bf16[2,4,8,24,768]{4,3,2,1,0:T(8,128)(2,1)}) custom-call(bf16[12,128,64]{2,1,0:T(8,128)(2,1)} %copy-done.5, bf16[128,768]{1,0:T(8,128)(2,1)} %bitcast.11, ...), custom_call_target="tpu_custom_call" | custom-call | tf_op jit(solution)/shard_map/experts_and_norms/pallas_call | solution.py:748
  132.3 0.0 copy-start.1
  132.4 69.5 %attention_backward.1 = (bf16[128,768]{1,0:T(8,128)(2,1)}, f32[24,1]{1,0:T(8,128)}, f32[24,768]{1,0:T(8,128)}, f32[24,768]{1,0:T(8,128)}, f32[24,768]{1,0:T(8,12...) custom-call(bf16[12,128,64]{2,1,0:T(8,128)(2,1)} %get-tuple-element.37.gatt_ref, ...), custom_call_target="tpu_custom_call" | custom-call | tf_op jit(solution)/shard_map/attention_backward/pallas_call | solution.py:1093
  201.9 1.3 reduce
  203.2 1.3 reduce.1
  204.5 1.4 copy.30
  205.9 0.0 copy-done.1
  205.9 0.0 copy-start.11
  205.9 0.0 copy-start.12
  205.9 0.0 copy-start.16
  205.9 0.0 copy-start.15
  205.9 0.0 copy-start.14
  205.9 0.0 copy-start.13
  206.0 0.0 copy-start.17
  206.0 23.2 %expert_weight_grads.1 = (f32[1,768,3072]{2,1,0:T(8,128)}, f32[1,3072,768]{2,1,0:T(8,128)}) custom-call(bf16[2,4,8,24,768]{4,3,2,1,0:T(8,128)(2,1)S(1)} %copy-done.1, bf16[1,768,3072]{2,1,0:T(8,128)(2,1)} %win_ref.3, bf16[1,3072,768]{2,1,0:T(8,128)(2,1)} %wout_ref.3), custom_call_target="tpu_custom_call" | custom-call | tf_op jit(solution)/shard_map/expert_weight_grads/pallas_call | solution.py:1176
  229.2 0.0 copy-done.11
  229.2 0.7 copy.38
  229.8 0.0 copy-done.12
  229.8 0.7 copy.39
  230.5 0.0 copy-done.16
  230.5 0.6 copy.40
  231.2 0.0 copy-done.15
  231.2 0.6 copy.41
  231.8 0.0 copy-done.14
  231.8 0.6 copy.42
  232.4 0.0 copy-done.13
  232.4 0.6 copy.43
  233.1 0.0 copy-done.17
  233.1 0.5 copy.44
Async XLA Ops:
  2.7 0.9 copy-start.2
  3.7 0.8 copy-start.6
  4.4 0.8 copy-start.7
  5.2 0.8 copy-start.8
  6.0 0.8 copy-start.9
  6.7 0.7 copy-start.10
  83.9 1.7 copy-start
  85.6 1.0 copy-start.3
  86.6 1.0 copy-start.4
  87.6 0.8 copy-start.5
  132.3 73.6 %copy-start.1 = (bf16[2,4,8,24,768]{4,3,2,1,0:T(8,128)(2,1)S(1)}, bf16[2,4,8,24,768]{4,3,2,1,0:T(8,128)(2,1)}, u32[]{:S(2)}) copy-start(bf16[2,4,8,24,768]{4,3,2,1,0:T(8,128)(2,1)} %get-tuple-element.53.slots_ref) | copy-start | bytes 7077892
  205.9 23.3 %copy-start.11 = (bf16[128,768]{1,0:T(8,128)(2,1)S(1)}, bf16[128,768]{1,0:T(8,128)(2,1)}, u32[]{:S(2)}) copy-start(bf16[128,768]{1,0:T(8,128)(2,1)} %get-tuple-element.36) | copy-start | bytes 589828
  205.9 23.9 %copy-start.12 = (bf16[128,768]{1,0:T(8,128)(2,1)S(1)}, bf16[128,768]{1,0:T(8,128)(2,1)}, u32[]{:S(2)}) copy-start(bf16[128,768]{1,0:T(8,128)(2,1)} %get-tuple-element.44) | copy-start | bytes 589828
  205.9 24.6 %copy-start.16 = (f32[24,768]{1,0:T(8,128)S(1)}, f32[24,768]{1,0:T(8,128)}, u32[]{:S(2)}) copy-start(f32[24,768]{1,0:T(8,128)} %get-tuple-element.95) | copy-start | bytes 221188
  205.9 25.2 %copy-start.15 = (f32[24,768]{1,0:T(8,128)S(1)}, f32[24,768]{1,0:T(8,128)}, u32[]{:S(2)}) copy-start(f32[24,768]{1,0:T(8,128)} %get-tuple-element.96) | copy-start | bytes 221188
  205.9 25.9 %copy-start.14 = (f32[24,768]{1,0:T(8,128)S(1)}, f32[24,768]{1,0:T(8,128)}, u32[]{:S(2)}) copy-start(f32[24,768]{1,0:T(8,128)} %get-tuple-element.97) | copy-start | bytes 221188
  205.9 26.5 %copy-start.13 = (f32[24,768]{1,0:T(8,128)S(1)}, f32[24,768]{1,0:T(8,128)}, u32[]{:S(2)}) copy-start(f32[24,768]{1,0:T(8,128)} %get-tuple-element.98) | copy-start | bytes 221188
  206.0 27.1 %copy-start.17 = (f32[1,12]{1,0:T(1,128)S(1)}, f32[1,12]{1,0:T(1,128)}, u32[]{:S(2)}) copy-start(f32[1,12]{1,0:T(1,128)} %get-tuple-element.50) | copy-start | bytes 148
